TPU v7x, 256 devices: a whole 4x4x8 slice. The times are simulated.
256 devices in a mesh: dp: 4 (over y), mp: 64 (over x, z, core).
Axes of the slice: x: 4, y: 4, z: 8, core: 2. Of those that a mesh axis runs over, the one named last changes fastest.
Arguments:
- grad_parts: bfloat16 [4, 2, 16384, 8192], P('dp', None, 'mp'), may hold values from -9 to 9
- omega: bfloat16 [8192, 512], P('dp'), may hold values from -0.0625 to 0.0625
- first_moment: float32 [512, 2, 8192], P('mp', None, 'dp'), may hold values from -0.75 to 0.75
- second_moment: float32 [512, 2, 8192], P('mp', None, 'dp'), may hold values from 0.0005 to 0.02
Outputs:
- new_first: float32 [512, 2, 8192], P('mp', None, 'dp')
- new_second: float32 [512, 2, 8192], P('mp', None, 'dp')
- weight_delta: bfloat16 [2, 16384, 8192], P(None, 'mp', 'dp')
All inputs are finite; a program needn't handle non-finite values.
Results may differ from a plain program's by a relative error of at most 0.03.
Values may be sent and summed in bfloat16 or wider, within the bound.
A program may use at most 128 MiB of HBM per device.

v0:
```python
import jax
import jax.numpy as jnp
from jax import lax
from jax.sharding import PartitionSpec as P

LAYERS = 2


def refresh(partial_value, omega, first_moment, second_moment):
    terms = partial_value.astype(jnp.float32)
    summed = lax.psum_scatter(terms.astype(jnp.bfloat16), "dp", scatter_dimension=2, tiled=True)
    local_panel = jnp.einsum("lrd,dk->lrk", summed, omega, preferred_element_type=jnp.float32)
    panel = lax.psum(local_panel.astype(jnp.bfloat16), "dp").astype(jnp.float32)
    gram_local = jnp.einsum("lrk,lrj->lkj", panel, panel, precision=lax.Precision.HIGHEST)
    gram = lax.psum(gram_local, "mp")
    lower = jnp.linalg.cholesky(gram)
    basis = lax.linalg.triangular_solve(lower, panel, left_side=False, lower=True, transpose_a=True)
    basis = basis.astype(jnp.bfloat16)
    columns = basis
    projected = lax.psum_scatter(
        jnp.einsum("lrk,lrd->kld", columns, summed, preferred_element_type=jnp.float32),
        "mp",
        scatter_dimension=0,
        tiled=True,
    )
    fresh_first = 0.9 * first_moment + 0.1 * projected
    fresh_second = 0.999 * second_moment + 0.001 * projected * projected
    normalized = (fresh_first / (jnp.sqrt(fresh_second) + 1e-08)).astype(jnp.bfloat16)
    columns = basis
    delta = jnp.einsum(
        "lrk,kld->lrd",
        columns,
        lax.all_gather(normalized, "mp", axis=0, tiled=True),
        preferred_element_type=jnp.float32,
    )
    return (fresh_first, fresh_second, delta.astype(jnp.bfloat16))


def local(grad_parts, omega, first_moment, second_moment):
    partial_value = grad_parts[0]
    results = []
    for layer_index in range(LAYERS):
        results.append(
            refresh(
                partial_value[layer_index : layer_index + 1],
                omega,
                first_moment[:, layer_index : layer_index + 1],
                second_moment[:, layer_index : layer_index + 1],
            )
        )
    new_first = jnp.concatenate([result[0] for result in results], axis=1)
    new_second = jnp.concatenate([result[1] for result in results], axis=1)
    weight_delta = jnp.concatenate([result[2] for result in results], axis=0)
    return (new_first, new_second, weight_delta)


def solution(mesh):
    return jax.shard_map(
        local,
        mesh=mesh,
        in_specs=(
            P("dp", None, "mp", None),
            P("dp", None),
            P("mp", None, "dp"),
            P("mp", None, "dp"),
        ),
        out_specs=(P("mp", None, "dp"), P("mp", None, "dp"), P(None, "mp", "dp")),
        check_vma=False,
    )
```

profile of v0, /device:TPU:1, one launch (start us, length us, event | category | flops | bytes accessed | tf_op | source)
XLA Modules:
  0.0 995.8 jit_solution(8381060138014672117)
XLA Ops:
  7.2 6.0 slice_bitcast_fusion.1
  14.0 52.6 %reduce-scatter.5.cloned.1.call-done = bf16[1,256,2048]{2,1,0:T(8,128)(2,1)} async-done(((bf16[1,256,8192]{2,1,0:T(8,128)(2,1)}), bf16[1,256,2048]{2,1,0:T(8,128)(2,1)}) %reduce-scatter.5.cloned.1.call-update) | async-done | bytes 1048592 | tf_op jit(solution)/shard_map/reduce_scatter | solution.py:11
  66.6 2.6 fusion.4
  69.3 49.2 %reduce-scatter.9.cloned.1.call-done = bf16[1,256,2048]{2,1,0:T(8,128)(2,1)} async-done(((bf16[1,256,8192]{2,1,0:T(8,128)(2,1)}), bf16[1,256,2048]{2,1,0:T(8,128)(2,1)}) %reduce-scatter.9.cloned.1.call-update) | async-done | bytes 1048592 | tf_op jit(solution)/shard_map/reduce_scatter | solution.py:11
  118.5 2.6 fusion.5
  121.2 46.4 %all-reduce.8.cloned.1.call-done = (bf16[1,256,512]{2,1,0:T(8,128)(2,1)}, bf16[1,256,512]{2,1,0:T(8,128)(2,1)}) async-done(((bf16[1,256,512]{2,1,0:T(8,128)(2,1)}, bf16[1,256,512]{2,1,0:T(8,128)(2,1)}), (bf16[1,256,512]{2,1,0:T(8,128)(2,1)}, bf16[1,256,512]{2,1,0:T(8,128)(2,1)})) %all-reduce.8.cloned.1.call-update) | async-done | bytes 524304 | tf_op jit(solution)/shard_map/psum | solution.py:13
  167.7 2.4 convolution_bitcast_fusion.2
  170.0 2.4 convolution_bitcast_fusion.3
  173.3 189.6 %all-reduce.6.cloned.1.call-done = (f32[1,512,512]{1,2,0:T(8,128)}, f32[1,512,512]{1,2,0:T(8,128)}) async-done(((f32[1,512,512]{1,2,0:T(8,128)}, f32[1,512,512]{1,2,0:T(8,128)}), (f32[1,512,512]{1,2,0:T(8,128)}, f32[1,512,512]{1,2,0:T(8,128)})) %all-reduce.6.cloned.1.call-update) | async-done | bytes 2097168 | tf_op jit(solution)/shard_map/psum | solution.py:15
  362.9 2.6 copy.12
  365.6 2.5 copy.9
  368.1 3.3 fusion.28
  372.4 11.7 %custom-call.35 = f32[1,128,128]{2,1,0:T(8,128)S(1)} custom-call(f32[1,128,128]{2,1,0:T(8,128)S(1)} %cholesky.425), custom_call_target="Cholesky" | custom-call | tf_op jit(solution)/shard_map/jit(cholesky)/cholesky | solution.py:16
  384.2 9.8 custom-call.36
  394.1 1.2 constant_dynamic-update-slice_fusion.7
  395.3 1.3 fusion.6
  396.6 11.7 %custom-call.37 = f32[1,128,128]{2,1,0:T(8,128)S(1)} custom-call(f32[1,128,128]{2,1,0:T(8,128)S(1)} %cholesky.429), custom_call_target="Cholesky" | custom-call | tf_op jit(solution)/shard_map/jit(cholesky)/cholesky | solution.py:16
  409.7 10.2 %custom-call.38 = f32[1,1,128,128]{2,3,1,0:T(8,128)S(1)} custom-call(f32[1,1,128,128]{3,2,1,0:T(8,128)S(1)} %get-tuple-element.66), custom_call_target="InvertDiagBlocksLowerTriangular" | custom-call | tf_op jit(solution)/shard_map/jit(cholesky)/cholesky | solution.py:16
  420.2 1.3 fusion.14
  421.5 11.7 %custom-call.39 = f32[1,128,128]{2,1,0:T(8,128)S(1)} custom-call(f32[1,128,128]{2,1,0:T(8,128)S(1)} %cholesky.434), custom_call_target="Cholesky" | custom-call | tf_op jit(solution)/shard_map/jit(cholesky)/cholesky | solution.py:16
  433.9 9.8 custom-call.40
  445.2 11.9 %custom-call.41 = f32[1,128,128]{2,1,0:T(8,128)S(1)} custom-call(f32[1,128,128]{2,1,0:T(8,128)S(1)} %fusion.26), custom_call_target="Cholesky" | custom-call | tf_op jit(solution)/shard_map/jit(cholesky)/cholesky | solution.py:16
  461.4 11.6 %while.4 = (s32[]{:T(128)}, f32[1,512,512]{2,1,0:T(8,128)}, s32[4,2]{0,1:T(2,128)S(1)}, f32[4,1,128,128]{3,2,1,0:T(8,128)S(1)}, s32[]{:T(128)}) while((s32[]{:T(128)}, f32[1,512,512]{2,1,0:T(8,128)}, s32[4,2]{0,1:T(2,128)S(1)}, f32[4,1,128,128]{3,2,1,0:T(8,128)S(1)}, s32[]{:T(128)}) %tuple.68), condition=%wide.while_cond, body=%wide.while_body.sunk | while | flops 2 | bytes 131181 | solution.py:17
  462.0 2.3 bitcast_dynamic-update-slice_fusion.4
  465.0 2.3 bitcast_dynamic-update-slice_fusion.4
  467.9 2.3 bitcast_dynamic-update-slice_fusion.4
  470.8 2.2 bitcast_dynamic-update-slice_fusion.4
  473.0 39.3 %custom-call.42 = f32[1,4,128,128]{2,3,1,0:T(8,128)S(1)} custom-call(f32[1,4,128,128]{3,2,1,0:T(8,128)S(1)} %bitcast.361), custom_call_target="InvertDiagBlocksLowerTriangular" | custom-call | tf_op jit(solution)/shard_map/triangular_solve/custom-call.3 | solution.py:17
  512.4 1.3 fusion.53
  513.7 1.3 fusion.11
  515.3 1.5 fusion.16
  517.2 1.8 fusion.21
  519.3 2.7 convolution_bitcast_fusion.1
  524.6 11.7 %custom-call.43 = f32[1,128,128]{2,1,0:T(8,128)S(1)} custom-call(f32[1,128,128]{2,1,0:T(8,128)S(1)} %cholesky.438), custom_call_target="Cholesky" | custom-call | tf_op jit(solution)/shard_map/jit(cholesky)/cholesky | solution.py:16
  536.4 9.8 custom-call.44
  546.3 1.2 constant_dynamic-update-slice_fusion.3
  547.6 1.3 fusion.7
  549.5 11.7 %custom-call.45 = f32[1,128,128]{2,1,0:T(8,128)S(1)} custom-call(f32[1,128,128]{2,1,0:T(8,128)S(1)} %cholesky.442), custom_call_target="Cholesky" | custom-call | tf_op jit(solution)/shard_map/jit(cholesky)/cholesky | solution.py:16
  561.3 10.2 %custom-call.46 = f32[1,1,128,128]{2,3,1,0:T(8,128)S(1)} custom-call(f32[1,1,128,128]{3,2,1,0:T(8,128)S(1)} %get-tuple-element.76), custom_call_target="InvertDiagBlocksLowerTriangular" | custom-call | tf_op jit(solution)/shard_map/jit(cholesky)/cholesky | solution.py:16
  572.6 1.3 fusion.17
  574.6 13.2 %custom-call.47 = f32[1,128,128]{2,1,0:T(8,128)} custom-call(f32[1,128,128]{2,1,0:T(8,128)} %cholesky.447), custom_call_target="Cholesky" | custom-call | tf_op jit(solution)/shard_map/jit(cholesky)/cholesky | solution.py:16
  587.8 1.5 select_reduce_fusion.1
  589.2 11.3 %custom-call.48 = f32[1,1,128,128]{2,3,1,0:T(8,128)} custom-call(f32[1,1,128,128]{3,2,1,0:T(8,128)} %get-tuple-element.73), custom_call_target="InvertDiagBlocksLowerTriangular" | custom-call | tf_op jit(solution)/shard_map/jit(cholesky)/cholesky | solution.py:16
  601.6 1.2 fusion.27
  602.8 11.7 %custom-call.49 = f32[1,128,128]{2,1,0:T(8,128)S(1)} custom-call(f32[1,128,128]{2,1,0:T(8,128)S(1)} %fusion.27), custom_call_target="Cholesky" | custom-call | tf_op jit(solution)/shard_map/jit(cholesky)/cholesky | solution.py:16
  620.8 11.7 %while.5 = (s32[]{:T(128)}, f32[1,512,512]{2,1,0:T(8,128)}, s32[4,2]{0,1:T(2,128)S(1)}, f32[4,1,128,128]{3,2,1,0:T(8,128)S(1)}, s32[]{:T(128)}) while((s32[]{:T(128)}, f32[1,512,512]{2,1,0:T(8,128)}, s32[4,2]{0,1:T(2,128)S(1)}, f32[4,1,128,128]{3,2,1,0:T(8,128)S(1)}, s32[]{:T(128)}) %tuple.89), condition=%wide.while_cond.clone, body=%wide.while_body.clone.sunk | while | flops 2 | bytes 131181 | solution.py:17
  621.6 2.3 bitcast_dynamic-update-slice_fusion.5
  624.5 2.3 bitcast_dynamic-update-slice_fusion.5
  627.4 2.3 bitcast_dynamic-update-slice_fusion.5
  630.3 2.2 bitcast_dynamic-update-slice_fusion.5
  632.6 39.3 %custom-call.50 = f32[1,4,128,128]{2,3,1,0:T(8,128)S(1)} custom-call(f32[1,4,128,128]{3,2,1,0:T(8,128)S(1)} %bitcast.360), custom_call_target="InvertDiagBlocksLowerTriangular" | custom-call | tf_op jit(solution)/shard_map/triangular_solve/custom-call.3 | solution.py:17
  671.9 1.3 fusion.52
  673.3 1.3 fusion.13
  675.0 1.5 fusion.19
  677.6 1.8 fusion.23
  680.6 2.7 convolution_bitcast_fusion
  684.5 1.5 divide_convert_fusion.1
  686.1 136.5 %reduce-scatter.11.cloned.1.call-done = f32[8,1,2048]{2,0,1:T(8,128)} async-done(((f32[512,1,2048]{2,0,1:T(8,128)}), f32[8,1,2048]{2,0,1:T(8,128)}) %reduce-scatter.11.cloned.1.call-update) | async-done | bytes 65552 | tf_op jit(solution)/shard_map/reduce_scatter | solution.py:20
  822.6 1.5 divide_convert_fusion
  825.7 81.3 %all-gather.3.cloned.1.call-done = bf16[512,1,2048]{2,0,1:T(8,128)(2,1)} async-done(((bf16[8,1,2048]{2,0,1:T(8,128)(2,1)}), bf16[512,1,2048]{2,0,1:T(8,128)(2,1)}) %all-gather.3.cloned.1.call-update) | async-done | bytes 2097168 | tf_op jit(solution)/shard_map/all_gather | solution.py:33
  907.0 3.3 fusion
  910.3 74.5 %all-gather.5.cloned.1.call-done = bf16[512,1,2048]{2,0,1:T(8,128)(2,1)} async-done(((bf16[8,1,2048]{2,0,1:T(8,128)(2,1)}), bf16[512,1,2048]{2,0,1:T(8,128)(2,1)}) %all-gather.5.cloned.1.call-update) | async-done | bytes 2097168 | tf_op jit(solution)/shard_map/all_gather | solution.py:33
  984.8 2.4 fusion.1
  987.2 1.5 pad_maximum_fusion
  (120 shorter events, 29.8 us)
Async XLA Ops:
  7.2 59.5 %copy-start = (bf16[2048,512]{1,0:T(8,128)(2,1)S(1)}, bf16[2048,512]{1,0:T(8,128)(2,1)}, u32[]{:S(2)}) copy-start(bf16[2048,512]{1,0:T(8,128)(2,1)} %param.8) | copy-start | bytes 6291460
  7.2 59.5 %reduce-scatter.5.cloned.1.call-start = ((), (), s32[]{:S(2)}) async-start(), calls=%async_computation.4 | async-start | bytes 5242880 | tf_op jit(solution)/shard_map/reduce_scatter | solution.py:11
  13.2 105.3 %reduce-scatter.9.cloned.1.call-start = ((), (), s32[]{:S(2)}) async-start(), calls=%async_computation.6 | async-start | bytes 5242880 | tf_op jit(solution)/shard_map/reduce_scatter | solution.py:11
  14.0 153.7 %all-reduce.8.cloned.1.call-start = ((), (), s32[]{:S(2)}) async-start(), calls=%async_computation.11 | async-start | bytes 1048576 | tf_op jit(solution)/shard_map/psum | solution.py:13
  121.2 241.8 %all-reduce.6.cloned.1.call-start = ((), (), s32[]{:S(2)}) async-start(), calls=%async_computation.10 | async-start | bytes 4194304 | tf_op jit(solution)/shard_map/psum | solution.py:15
  167.7 4.8 copy-start.10
  172.4 512.1 %reduce-scatter.7.cloned.1.call-start = ((), (), s32[]{:S(2)}) async-start(), calls=%async_computation.5 | async-start | bytes 4259840 | tf_op jit(solution)/shard_map/reduce_scatter | solution.py:20
  362.9 5.2 copy-start.2
  371.4 1.0 copy-start.3
  461.4 54.0 %copy-start.7 = (f32[1,256,512]{2,1,0:T(8,128)S(1)}, f32[1,256,512]{2,1,0:T(8,128)}, u32[]{:S(2)}) copy-start(f32[1,256,512]{2,1,0:T(8,128)} %convert_element_type.48) | copy-start | bytes 1572868
  512.3 7.0 copy-start.12
  517.2 4.8 copy-start.4
  519.3 2.7 copy-start.14
  522.0 1.0 copy-start.9
  522.0 300.6 %reduce-scatter.11.cloned.1.call-start = ((), (), s32[]{:S(2)}) async-start(), calls=%async_computation.7 | async-start | bytes 4259840 | tf_op jit(solution)/shard_map/reduce_scatter | solution.py:20
  548.8 0.7 copy-start.13
  620.8 54.1 %copy-start.8 = (f32[1,256,512]{2,1,0:T(8,128)S(1)}, f32[1,256,512]{2,1,0:T(8,128)}, u32[]{:S(2)}) copy-start(f32[1,256,512]{2,1,0:T(8,128)} %convert_element_type.52) | copy-start | bytes 1572868
  671.9 3.0 copy-start.17
  671.9 8.7 copy-start.11
  677.6 5.7 copy-start.6
  680.6 2.7 copy-start.16
  683.3 0.9 copy-start.18
  683.3 1.0 copy-start.19
  683.3 223.7 %copy-start.5 = (f32[1,256,128]{1,2,0:T(8,128)S(1)}, f32[1,256,128]{1,2,0:T(8,128)}, u32[]{:S(2)}) copy-start(f32[1,256,128]{1,2,0:T(8,128)} %copy-done.4) | copy-start | bytes 393220
  683.3 223.7 %copy-start.15 = (bf16[1,256,128]{1,2,0:T(8,128)(2,1)S(1)}, bf16[1,256,128]{1,2,0:T(8,128)(2,1)}, u32[]{:S(2)}) copy-start(bf16[1,256,128]{1,2,0:T(8,128)(2,1)} %copy-done.14) | copy-start | bytes 196612
  683.4 223.7 %all-gather.3.cloned.1.call-start = ((), (), s32[]{:S(2)}) async-start(), calls=%async_computation.8 | async-start | bytes 2129920 | tf_op jit(solution)/shard_map/all_gather | solution.py:33
  686.1 298.7 %all-gather.5.cloned.1.call-start = ((), (), s32[]{:S(2)}) async-start(), calls=%async_computation.9 | async-start | bytes 2129920 | tf_op jit(solution)/shard_map/all_gather | solution.py:33
  910.3 76.9 %copy-start.1 = (bf16[1,256,2048]{2,1,0:T(8,128)(2,1)S(1)}, bf16[1,256,2048]{2,1,0:T(8,128)(2,1)}, u32[]{:S(2)}) copy-start(bf16[1,256,2048]{2,1,0:T(8,128)(2,1)} %fusion) | copy-start | bytes 3145732
Sparse Core Ops, SparseCore 0:
  13.4 53.2 reduce-scatter.4
  69.4 49.1 reduce-scatter.8
  121.5 46.0 all-reduce.7
  172.5 190.3 all-reduce.5
  522.1 140.1 reduce-scatter.6
  683.5 139.1 reduce-scatter.10
  826.0 81.0 all-gather.2
  909.8 74.9 all-gather.4
where the time goes:
time: 1010 us; the launch traced here: 996 us
  waiting for transfers between devices  631 us (62%)
  other arithmetic  254 us (25%)
  matrix products  49.2 us (5%)
  local copies, waits for them, and re-layouts  41.1 us (4%)
  between operations  20 us (2%)
    psum x1, waiting for transfers between devices, refresh(): gram = lax.psum(gram_local, 'mp')  190 us
    another operation x30, other arithmetic, refresh(): lower = jnp.linalg.cholesky(gram)  163 us
    all_gather x2, waiting for transfers between devices, refresh(): lax.all_gather(normalized, 'mp', axis=0, tiled=True)  156 us
    reduce_scatter x2, waiting for transfers between devices, refresh(): lax.psum_scatter(jnp.einsum('lrk,lrd->kld', columns, summed, preferred_el...  137 us
    reduce_scatter x2, waiting for transfers between devices, refresh(): lax.psum_scatter(terms.astype(jnp.bfloat16), 'dp', scatter_dimension=2, t...  102 us
    another operation x5, other arithmetic, refresh(): lax.linalg.triangular_solve(lower, panel, left_side=False, lower=True, tr...  80.8 us
    psum x1, waiting for transfers between devices, refresh(): panel = lax.psum(local_panel.astype(jnp.bfloat16), 'dp').astype(jnp.float32)  46.4 us
    another operation x27, local copies, waits for them, and re-layouts, refresh(): lax.linalg.triangular_solve(lower, panel, left_side=False, lower=True, tr...  23.1 us
  transfers between devices with their start and end apart: 8, of which 7 were waited for; matrix products, arithmetic and copies ran while one was open for 17% of the time, Pallas kernels for 0%

commit v1 on v0

v1 whole, which is shorter than its diff:
```python
import functools

import jax
import jax.numpy as jnp
from jax import lax
from jax.experimental import pallas as pl
from jax.experimental.pallas import tpu as pltpu
from jax.sharding import PartitionSpec as P

HIGHEST = lax.Precision.HIGHEST
MESH = pl.DeviceIdType.MESH
NT = (((1,), (1,)), ((), ()))
TN = (((0,), (0,)), ((), ()))
BF = jnp.bfloat16
F32 = jnp.float32

LAYERS = 2
ROWS = 256
D = 8192
OWN = 2048
HALF = 1024
RANK = 512
B = 128
NY, NX, NZ, NC = 4, 4, 8, 2


def place():
    mp = lax.axis_index("mp")
    return lax.axis_index("dp"), mp // (NZ * NC), (mp // NC) % NZ, mp % NC


def device(y, x, z, c):
    return {"dp": y, "mp": x * (NZ * NC) + z * NC + c}


def greet(peers):
    barrier = pltpu.get_barrier_semaphore()
    for peer in peers:
        pl.semaphore_signal(barrier, inc=1, device_id=peer, device_id_type=MESH)
    pl.semaphore_wait(barrier, len(peers))


def along(axis, spot, k):
    y, x, z, c = spot
    if axis == "y":
        return device((y + k) % NY, x, z, c)
    if axis == "x":
        return device(y, (x + k) % NX, z, c)
    if axis == "z":
        return device(y, x, (z + k) % NZ, c)
    return device(y, x, z, 1 - c)


def ship(src, dst, send, recv, peer):
    copy = pltpu.make_async_remote_copy(
        src_ref=src, dst_ref=dst, send_sem=send, recv_sem=recv, device_id=peer, device_id_type=MESH
    )
    copy.start()
    return copy


def span(start, size):
    return pl.ds(pl.multiple_of(start, size), size)


def gram_kernel(part_ref, panel_ref, blocks_ref, rs_buf, mine, core_buf, chip, z_buf, strip, x_buf, sems):
    spot = place()
    y, x, z, c = spot
    peers = [along("y", spot, k) for k in range(1, NY)]
    peers += [along("z", spot, k) for k in range(1, NZ)]
    peers += [along("x", spot, k) for k in range(1, NX)]
    peers += [along("c", spot, 1)]
    greet(peers)
    done = []
    count = [0]

    def go(src, dst, peer):
        copy = ship(src, dst, sems.at[0, count[0]], sems.at[1, count[0]], peer)
        count[0] += 1
        done.append(copy)
        return copy

    q = ROWS // NY
    own = span(y * q, q)
    copies = [
        go(part_ref.at[:, span(((y + k) % NY) * q, q), :], rs_buf.at[k - 1], along("y", spot, k)) for k in range(1, NY)
    ]
    total = part_ref[:, own, :].astype(F32)
    for k, copy in enumerate(copies):
        copy.wait_recv()
        total = total + rs_buf[k].astype(F32)
    panel_ref[:, own, :] = total.astype(BF)
    copies = [go(panel_ref.at[:, own, :], panel_ref.at[:, own, :], along("y", spot, k)) for k in range(1, NY)]
    for copy in copies:
        copy.wait_recv()

    for b in range(5):
        low = (y - b + 4) // 4
        layer = 1 - low
        i = low * y + (1 - low) * (3 - y)
        j = low * b + (1 - low) * (b - y - 1)
        left = panel_ref[layer, :, span(i * B, B)]
        right = panel_ref[layer, :, span(j * B, B)]
        mine[b * B : b * B + B, :] = lax.dot_general(left, right, TN, preferred_element_type=F32)

    copy = go(mine.at[span((1 - c) * 320, 320), :], core_buf, along("c", spot, 1))
    copy.wait_recv()
    chip[...] = mine[span(c * 320, 320), :] + core_buf[...]
    copies = [
        go(chip.at[span(((z + k) % NZ) * 40, 40), :], z_buf.at[k - 1], along("z", spot, k)) for k in range(1, NZ)
    ]
    total = chip[span(z * 40, 40), :]
    for k, copy in enumerate(copies):
        copy.wait_recv()
        total = total + z_buf[k]
    strip[...] = total
    copies = [go(strip, x_buf.at[k - 1], along("x", spot, k)) for k in range(1, NX)]
    for k, copy in enumerate(copies):
        copy.wait_recv()
        total = total + x_buf[k]
    place_of = pl.ds(pl.multiple_of(c * 320 + z * 40, 8), 40)
    blocks_ref[y, place_of, :] = total
    piece = blocks_ref.at[y, place_of, :]
    copies = [go(piece, piece, along("z", spot, k)) for k in range(1, NZ)]
    for copy in copies:
        copy.wait_recv()
    piece = blocks_ref.at[y, span(c * 320, 320), :]
    copies = [go(piece, piece, along("y", spot, k)) for k in range(1, NY)]
    for copy in copies:
        copy.wait_recv()
    piece = blocks_ref.at[:, span(c * 320, 320), :]
    go(piece, piece, along("c", spot, 1)).wait_recv()
    for copy in done:
        copy.wait_send()


def gram(part):
    vmem = pl.BlockSpec(memory_space=pltpu.VMEM)
    return pl.pallas_call(
        gram_kernel,
        out_shape=(
            jax.ShapeDtypeStruct((LAYERS, ROWS, RANK), BF),
            jax.ShapeDtypeStruct((4, 640, B), F32),
        ),
        in_specs=[vmem],
        out_specs=(vmem, vmem),
        scratch_shapes=[
            pltpu.VMEM((NY - 1, LAYERS, ROWS // NY, RANK), BF),
            pltpu.VMEM((640, B), F32),
            pltpu.VMEM((320, B), F32),
            pltpu.VMEM((320, B), F32),
            pltpu.VMEM((NZ - 1, 40, B), F32),
            pltpu.VMEM((40, B), F32),
            pltpu.VMEM((NX - 1, 40, B), F32),
            pltpu.SemaphoreType.DMA((2, 32)),
        ],
        compiler_params=pltpu.CompilerParams(collective_id=0, has_side_effects=True, vmem_limit_bytes=32 << 20),
    )(part)


def eliminate(tiles):
    lane = lax.broadcasted_iota(jnp.int32, (8, B), 1)
    sub = lax.broadcasted_iota(jnp.int32, (8, B), 0)
    for j in range(B):
        first, at = divmod(j, 8)
        for rows in tiles:
            row = rows[first][at : at + 1, :]
            inverse = 1.0 / row[:, j : j + 1]
            scaled = jnp.where(lane == j, 1.0, jnp.broadcast_to(row, (8, B))) * inverse
            for t in range(first, B // 8):
                if t == first and at == 7:
                    continue
                column = jnp.broadcast_to(rows[t][:, j : j + 1], (8, B))
                new = jnp.where(lane == j, 0.0, rows[t]) - column * scaled
                rows[t] = jnp.where(sub > at, new, rows[t]) if t == first else new
    return tiles


def finish(rows):
    whole = jnp.concatenate(rows, axis=0)
    r = lax.broadcasted_iota(jnp.int32, (B, B), 0)
    q = lax.broadcasted_iota(jnp.int32, (B, B), 1)
    pivot = jnp.sum(jnp.where(r == q, whole, 0.0), axis=1, keepdims=True)
    return jnp.where(q < r, whole, jnp.where(q == r, 1.0, 0.0)) * lax.rsqrt(pivot)


def factor_kernel(blocks_ref, panel_ref, basis_ref, w):
    for i in range(4):
        for j in range(i + 1):
            for layer, (who, at) in enumerate(((i, j), (3 - i, 4 - i + j))):
                block = blocks_ref[who, at * B : at * B + B, :]
                w[layer, i * B : i * B + B, j * B : j * B + B] = block
                if i != j:
                    w[layer, j * B : j * B + B, i * B : i * B + B] = block.T

    def step(k, carry):
        here = span(k * B, B)
        tiles = [[w[n, span(k * B + 8 * t, 8), here] for t in range(B // 8)] for n in range(LAYERS)]
        tiles = eliminate(tiles)
        r = lax.broadcasted_iota(jnp.int32, (RANK, 1), 0)
        q = lax.broadcasted_iota(jnp.int32, (1, RANK), 1)
        eye = lax.broadcasted_iota(jnp.int32, (B, RANK), 0) + k * B == lax.broadcasted_iota(jnp.int32, (B, RANK), 1)
        inside = (q >= k * B) & (q < k * B + B)
        below = r >= k * B + B
        for n in range(LAYERS):
            inverse = finish(tiles[n])
            top = jnp.where(inside, eye.astype(F32), w[n, here, :])
            right = jnp.dot(inverse, top, precision=HIGHEST, preferred_element_type=F32)
            left = lax.dot_general(w[n, :, here], inverse, NT, precision=HIGHEST, preferred_element_type=F32)
            left = jnp.where(below, left, 0.0)
            rest = jnp.where(inside & below, 0.0, w[n])
            w[n] = rest - jnp.dot(left, right, precision=HIGHEST, preferred_element_type=F32)
            w[n, here, :] = jnp.where(q < k * B + B, right, 0.0)
        return carry

    lax.fori_loop(0, 4, step, 0)
    for n in range(LAYERS):
        basis = lax.dot_general(panel_ref[n].astype(F32), w[n], NT, precision=HIGHEST, preferred_element_type=F32)
        basis_ref[n] = basis.astype(BF)


def factor(blocks, panel):
    vmem = pl.BlockSpec(memory_space=pltpu.VMEM)
    return pl.pallas_call(
        factor_kernel,
        out_shape=jax.ShapeDtypeStruct((LAYERS, ROWS, RANK), BF),
        in_specs=[vmem, vmem],
        out_specs=vmem,
        scratch_shapes=[pltpu.VMEM((LAYERS, RANK, RANK), F32)],
        compiler_params=pltpu.CompilerParams(vmem_limit_bytes=32 << 20),
    )(blocks, panel)


def tail_kernel(
    basis_ref,
    summed_ref,
    first_ref,
    second_ref,
    new_first_ref,
    new_second_ref,
    delta_ref,
    twin_basis,
    twin_summed,
    x_out,
    x_in,
    x_own,
    z_out,
    z_in,
    z_own,
    full,
    fresh,
    joined,
    gathered,
    sems,
):
    spot = place()
    y, x, z, c = spot
    peers = [along("c", spot, 1)]
    peers += [along("x", spot, k) for k in range(1, NX)]
    peers += [along("z", spot, k) for k in range(1, NZ)]
    greet(peers)
    done = []
    count = [0]

    def go(src, dst, peer):
        copy = ship(src, dst, sems.at[0, count[0]], sems.at[1, count[0]], peer)
        count[0] += 1
        done.append(copy)
        return copy

    mine, other = span(c * HALF, HALF), span((1 - c) * HALF, HALF)
    twin = along("c", spot, 1)
    got = [
        (go(basis_ref.at[n], twin_basis.at[n], twin), go(summed_ref.at[n, :, other], twin_summed.at[n], twin))
        for n in range(LAYERS)
    ]

    def product(n, part):
        here = span(part * B, B)
        out = lax.dot_general(basis_ref[n, :, here], summed_ref[n, :, mine], TN, preferred_element_type=F32)
        return out + lax.dot_general(twin_basis[n, :, here], twin_summed[n], TN, preferred_element_type=F32)

    x_copies = []
    for n in range(LAYERS):
        for copy in got[n]:
            copy.wait_recv()
        copies = []
        for k in (2, 1, 3):
            x_out[n, k - 1] = product(n, (x + k) % NX).astype(BF)
            copies.append((k, go(x_out.at[n, k - 1], x_in.at[n, k - 1], along("x", spot, k))))
        x_own[n] = product(n, x)
        x_copies.append(copies)

    z_copies = []
    for n in range(LAYERS):
        for k, copy in x_copies[n]:
            copy.wait_recv()
        total = x_own[n]
        for k in range(1, NX):
            total = total + x_in[n, k - 1].astype(F32)
        x_own[n] = total
        z_out[n] = total.astype(BF)
        z_own[n] = x_own[n, span(z * 16, 16), :]
        z_copies.append(
            [go(z_out.at[n, span(((z + k) % NZ) * 16, 16), :], z_in.at[n, k - 1], along("z", spot, k)) for k in range(1, NZ)]
        )
    for n in range(LAYERS):
        total = z_own[n]
        for k, copy in enumerate(z_copies[n]):
            copy.wait_recv()
            total = total + z_in[n, k].astype(F32)
        z_own[n] = total

    copy = go(z_own.at[:, span((1 - c) * 8, 8), :], full.at[:, :, mine], twin)
    full[:, :, mine] = z_own[:, span(c * 8, 8), :]
    copy.wait_recv()
    for n in range(LAYERS):
        projected = full[n]
        new_first = 0.9 * first_ref[:, n, :] + 0.1 * projected
        new_second = 0.999 * second_ref[:, n, :] + 0.001 * projected * projected
        new_first_ref[:, n, :] = new_first
        new_second_ref[:, n, :] = new_second
        fresh[n] = new_first / (jnp.sqrt(new_second) + 1e-08)
    rows = span(c * 8, 8)
    copy = go(fresh.at[:, :, other], joined.at[:, rows, :], twin)
    joined[:, rows, :] = fresh[:, :, mine]
    copy.wait_recv()

    slot = span(x * B + z * 16, 16)
    gathered[c, :, slot, :] = joined[...].astype(BF)
    piece = gathered.at[c, :, slot, :]
    copies = [go(piece, piece, along("z", spot, k)) for k in range(1, NZ)]
    for copy in copies:
        copy.wait_recv()
    piece = gathered.at[c, :, span(x * B, B), :]
    copies = [(k, go(piece, piece, along("x", spot, k))) for k in (2, 1, 3)]
    crossed = [go(piece, piece, twin)]
    for k, copy in copies[1:] + copies[:1]:
        copy.wait_recv()
        piece = gathered.at[c, :, span(((x - k + NX) % NX) * B, B), :]
        crossed.append(go(piece, piece, twin))
    for copy in crossed:
        copy.wait_recv()

    tile = 256
    for n in range(LAYERS):
        for half in range(2):

            def body(t, carry):
                right = gathered[half, n, :, span(t * tile, tile)]
                out = jnp.dot(basis_ref[n], right, preferred_element_type=F32)
                delta_ref[n, :, span(half * HALF + t * tile, tile)] = out.astype(BF)
                return carry

            lax.fori_loop(0, HALF // tile, body, 0)
    for copy in done:
        copy.wait_send()


def tail(basis, summed, first, second):
    vmem = pl.BlockSpec(memory_space=pltpu.VMEM)
    return pl.pallas_call(
        tail_kernel,
        out_shape=(
            jax.ShapeDtypeStruct((8, LAYERS, OWN), F32),
            jax.ShapeDtypeStruct((8, LAYERS, OWN), F32),
            jax.ShapeDtypeStruct((LAYERS, ROWS, OWN), BF),
        ),
        in_specs=[vmem] * 4,
        out_specs=(vmem,) * 3,
        scratch_shapes=[
            pltpu.VMEM((LAYERS, ROWS, RANK), BF),
            pltpu.VMEM((LAYERS, ROWS, HALF), BF),
            pltpu.VMEM((LAYERS, NX - 1, B, HALF), BF),
            pltpu.VMEM((LAYERS, NX - 1, B, HALF), BF),
            pltpu.VMEM((LAYERS, B, HALF), F32),
            pltpu.VMEM((LAYERS, B, HALF), BF),
            pltpu.VMEM((LAYERS, NZ - 1, 16, HALF), BF),
            pltpu.VMEM((LAYERS, 16, HALF), F32),
            pltpu.VMEM((LAYERS, 8, OWN), F32),
            pltpu.VMEM((LAYERS, 8, OWN), F32),
            pltpu.VMEM((LAYERS, 16, HALF), F32),
            pltpu.VMEM((2, LAYERS, RANK, HALF), BF),
            pltpu.SemaphoreType.DMA((2, 48)),
        ],
        compiler_params=pltpu.CompilerParams(collective_id=1, has_side_effects=True, vmem_limit_bytes=48 << 20),
    )(basis, summed, first, second)


def local(grad_parts, omega, first_moment, second_moment):
    summed = lax.psum_scatter(grad_parts[0], "dp", scatter_dimension=2, tiled=True)
    part = jnp.einsum("lrd,dk->lrk", summed, omega, preferred_element_type=F32).astype(BF)
    panel, blocks = gram(part)
    basis = factor(blocks, panel)
    return tail(basis, summed, first_moment, second_moment)


def solution(mesh):
    return jax.shard_map(
        local,
        mesh=mesh,
        in_specs=(P("dp", None, "mp", None), P("dp", None), P("mp", None, "dp"), P("mp", None, "dp")),
        out_specs=(P("mp", None, "dp"), P("mp", None, "dp"), P(None, "mp", "dp")),
        check_vma=False,
    )
```

time: 1010 us -> 332 us (0.33); the launches traced: 996 us -> 331 us
  waiting for transfers between devices: 631 us -> 90.4 us
  other arithmetic: 254 us -> 0 us
  Pallas kernels: 0 us -> 221 us
  matrix products: 49.2 us -> 2.83 us
  local copies, waits for them, and re-layouts: 41.1 us -> 2.66 us
    another operation x35 -> x0, other arithmetic: 244 us -> none  [the longest x30 163 us: refresh(): lower = jnp.linalg.cholesky(gram)]
    psum x2 -> x0, waiting for transfers between devices: 236 us -> none  [the longest x1 190 us: refresh(): gram = lax.psum(gram_local, 'mp')]
    pallas_call x0 -> x3, Pallas kernels: none -> 221 us  [the longest x1 84.3 us: tail(): pl.pallas_call(tail_kernel, out_shape=(jax.ShapeDtypeStruct((8, LAYERS, O...]
    all_gather x2 -> x0, waiting for transfers between devices: 156 us -> none  [refresh(): lax.all_gather(normalized, 'mp', axis=0, tiled=True)]
    reduce_scatter x4 -> x1, waiting for transfers between devices: 238 us -> 89.7 us  [local(): lax.psum_scatter(grad_parts[0], 'dp', scatter_dimension=2, tiled=True)]
    another operation x26 -> x0, matrix products: 28.1 us -> none  [the longest x14 15.5 us: refresh(): lax.linalg.triangular_solve(lower, panel, left_side=False, lower=True, tr...]
    another operation x35 -> x0, local copies, waits for them, and re-layouts: 24.8 us -> none  [the longest x27 23.1 us: refresh(): lax.linalg.triangular_solve(lower, panel, left_side=False, lower=True, tr...]
    dot_general x8 -> x1, matrix products: 21.1 us -> 2.83 us  [local(): jnp.einsum('lrd,dk->lrk', summed, omega, preferred_element_type=F32)]
  transfers between devices with their start and end apart: 8 -> 1, of which waited for: 7 -> 1; matrix products, arithmetic and copies ran while one was open for 17% -> 0% of each run, Pallas kernels for 0% -> 0%
where the time goes in v1:
time: 332 us; the launch traced here: 331 us
  Pallas kernels  221 us (67%)
  waiting for transfers between devices  90.4 us (27%)
  between operations  14.1 us (4%)
    reduce_scatter x1, waiting for transfers between devices, local(): lax.psum_scatter(grad_parts[0], 'dp', scatter_dimension=2, tiled=True)  89.7 us
    pallas_call x1, Pallas kernels, tail(): pl.pallas_call(tail_kernel, out_shape=(jax.ShapeDtypeStruct((8, LAYERS, O...  84.3 us
    pallas_call x1, Pallas kernels, factor(): pl.pallas_call(factor_kernel, out_shape=jax.ShapeDtypeStruct((LAYERS, ROW...  84.2 us
    pallas_call x1, Pallas kernels, gram(): pl.pallas_call(gram_kernel, out_shape=(jax.ShapeDtypeStruct((LAYERS, ROWS...  52.3 us
  transfers between devices with their start and end apart: 1, of which 1 were waited for; matrix products, arithmetic and copies ran while one was open for 0% of the time, Pallas kernels for 0%

profile of v1, /device:TPU:1, one launch (start us, length us, event | category | flops | bytes accessed | tf_op | source)
XLA Modules:
  0.0 330.8 jit_solution(9020455129621988530)
XLA Ops:
  7.2 0.0 copy-start
  7.2 0.0 reduce-scatter.2.cloned.1.call-start
  7.2 0.7 reduce-scatter.2.cloned.1.call-update
  7.9 89.7 %reduce-scatter.2.cloned.1.call-done.summed_ref = bf16[2,256,2048]{2,1,0:T(8,128)(2,1)} async-done(((bf16[2,256,8192]{2,1,0:T(8,128)(2,1)}), bf16[2,256,2048]{2,1,0:T(8,128)(2,1)}) %reduce-scatter.2.cloned.1.call-update) | async-done | bytes 2097168 | tf_op jit(solution)/shard_map/reduce_scatter | solution.py:391
  97.6 0.0 copy-done
  97.6 2.8 fusion.2.part_ref
  100.4 0.0 copy-start.1
  100.4 0.0 copy-start.2
  100.5 0.0 copy-start.3
  100.5 52.3 %shard_map.67 = (bf16[2,256,512]{2,1,0:T(8,128)(2,1)S(1)}, f32[4,640,128]{2,1,0:T(8,128)S(1)}) custom-call(bf16[2,256,512]{2,1,0:T(8,128)(2,1)S(1)} %fusion.2.part_ref), custom_call_target="tpu_custom_call" | custom-call | tf_op jit(solution)/shard_map/pallas_call | solution.py:139
  152.8 84.2 %shard_map.68.basis_ref = bf16[2,256,512]{2,1,0:T(8,128)(2,1)S(1)} custom-call(f32[4,640,128]{2,1,0:T(8,128)S(1)} %get-tuple-element.5.blocks_ref, bf16[2,256,512]{2,1,0:T(8,128)(2,1)S(1)} %get-tuple-element.6.panel_ref), custom_call_target="tpu_custom_call" | custom-call | tf_op jit(solution)/shard_map/pallas_call | solution.py:224
  237.0 0.0 copy-done.1
  237.0 0.0 copy-done.2
  237.0 0.0 copy-done.3
  237.0 84.3 %shard_map.69 = (f32[8,2,2048]{2,1,0:T(2,128)S(1)}, f32[8,2,2048]{2,1,0:T(2,128)S(1)}, bf16[2,256,2048]{2,1,0:T(8,128)(2,1)S(1)}) custom-call(bf16[2,256,512]{2,1,0:T(8,128)(2,1)S(1)} %shard_map.68.basis_ref, bf16[2,256,2048]{2,1,0:T(8,128)(2,1)S(1)} %copy-done.1, f32[8,2,2048]{2,1,0:T(2,128)S(1)} %copy-done.2, f32[8,2,2048]{2,1,0:T(2,128)S(1)} %copy-done.3), custom_call_target="tpu_custom_call" | custom-call | tf_op jit(solution)/shard_map/pallas_call | solution.py:362
  321.3 0.7 copy.10
  322.0 0.7 copy.11
  322.7 1.3 copy.12
Async XLA Ops:
  7.2 90.4 %copy-start = (bf16[2048,512]{1,0:T(8,128)(2,1)S(1)}, bf16[2048,512]{1,0:T(8,128)(2,1)}, u32[]{:S(2)}) copy-start(bf16[2048,512]{1,0:T(8,128)(2,1)} %param.5) | copy-start | bytes 6291460
  7.2 90.4 %reduce-scatter.2.cloned.1.call-start = ((), (), s32[]{:S(2)}) async-start(), calls=%async_computation.1 | async-start | bytes 10485760 | tf_op jit(solution)/shard_map/reduce_scatter | solution.py:391
  100.4 136.5 %copy-start.1 = (bf16[2,256,2048]{2,1,0:T(8,128)(2,1)S(1)}, bf16[2,256,2048]{2,1,0:T(8,128)(2,1)}, u32[]{:S(2)}) copy-start(bf16[2,256,2048]{2,1,0:T(8,128)(2,1)} %reduce-scatter.2.cloned.1.call-done.summed_ref) | copy-start | bytes 6291460
  100.4 136.5 %copy-start.2 = (f32[8,2,2048]{2,1,0:T(2,128)S(1)}, f32[8,2,2048]{2,1,0:T(2,128)}, u32[]{:S(2)}) copy-start(f32[8,2,2048]{2,1,0:T(2,128)} %first_ref.1) | copy-start | bytes 393220
  100.5 136.5 %copy-start.3 = (f32[8,2,2048]{2,1,0:T(2,128)S(1)}, f32[8,2,2048]{2,1,0:T(2,128)}, u32[]{:S(2)}) copy-start(f32[8,2,2048]{2,1,0:T(2,128)} %second_ref.1) | copy-start | bytes 393220
Sparse Core Ops, SparseCore 0:
  10.6 86.9 reduce-scatter.1

commit v2 on v1

--- a/solution.py
+++ b/solution.py
@@ -61,6 +61,90 @@
 
 def span(start, size):
     return pl.ds(pl.multiple_of(start, size), size)
+
+
+def panel_kernel(omega_ref, grads_hbm, part_ref, grads, far, total, sems, local_sems):
+    spot = place()
+    y, x, z, c = spot
+    up, down, twin = along("y", spot, 1), along("y", spot, NY - 1), along("c", spot, 1)
+    order = (0, NY - 1, 1, 2)
+    loads = []
+    for k in order:
+        columns = span(((y + k) % NY) * OWN, OWN)
+        load = pltpu.make_async_copy(grads_hbm.at[:, :, columns], grads.at[k], local_sems.at[k])
+        load.start()
+        loads.append(load)
+    greet([up, down, twin])
+    done = []
+    count = [0]
+
+    def go(src, dst, peer):
+        copy = ship(src, dst, sems.at[0, count[0]], sems.at[1, count[0]], peer)
+        count[0] += 1
+        done.append(copy)
+        return copy
+
+    q = OWN // 4
+    rows = [span(c * 2 * q + h * q, q) for h in range(2)]
+    near = [None] * 4
+    near[0] = go(omega_ref.at[rows[0], :], far.at[0, rows[0], :], up)
+    near[1] = go(omega_ref.at[rows[1], :], far.at[1, rows[1], :], down)
+    near[2] = go(omega_ref.at[rows[1], :], far.at[0, rows[1], :], up)
+    near[3] = go(omega_ref.at[rows[0], :], far.at[1, rows[0], :], down)
+
+    def add(k, matrix, fresh):
+        for n in range(LAYERS):
+            out = jnp.dot(grads[k, n], matrix[...], preferred_element_type=F32)
+            total[n] = out if fresh else total[n] + out
+
+    loads[0].wait()
+    add(0, omega_ref, True)
+    near[0].wait_recv()
+    relay = [go(far.at[0, rows[0], :], far.at[2, rows[0], :], up)]
+    crossed = [go(far.at[0, rows[0], :], far.at[0, rows[0], :], twin)]
+    near[1].wait_recv()
+    relay.append(go(far.at[1, rows[1], :], far.at[2, rows[1], :], down))
+    crossed.append(go(far.at[1, rows[1], :], far.at[1, rows[1], :], twin))
+    near[2].wait_recv()
+    crossed.append(go(far.at[0, rows[1], :], far.at[0, rows[1], :], twin))
+    near[3].wait_recv()
+    crossed.append(go(far.at[1, rows[0], :], far.at[1, rows[0], :], twin))
+    crossed[0].wait_recv()
+    crossed[2].wait_recv()
+    loads[1].wait()
+    add(NY - 1, far.at[0], False)
+    crossed[1].wait_recv()
+    crossed[3].wait_recv()
+    loads[2].wait()
+    add(1, far.at[1], False)
+    for h, copy in enumerate(relay):
+        copy.wait_recv()
+        crossed.append(go(far.at[2, rows[h], :], far.at[2, rows[h], :], twin))
+    crossed[4].wait_recv()
+    crossed[5].wait_recv()
+    loads[3].wait()
+    add(2, far.at[2], False)
+    part_ref[...] = total[...].astype(BF)
+    for copy in done:
+        copy.wait_send()
+
+
+def panel_part(omega, grads):
+    vmem = pl.BlockSpec(memory_space=pltpu.VMEM)
+    return pl.pallas_call(
+        panel_kernel,
+        out_shape=jax.ShapeDtypeStruct((LAYERS, ROWS, RANK), BF),
+        in_specs=[vmem, pl.BlockSpec(memory_space=pl.ANY)],
+        out_specs=vmem,
+        scratch_shapes=[
+            pltpu.VMEM((NY, LAYERS, ROWS, OWN), BF),
+            pltpu.VMEM((NY - 1, OWN, RANK), BF),
+            pltpu.VMEM((LAYERS, ROWS, RANK), F32),
+            pltpu.SemaphoreType.DMA((2, 12)),
+            pltpu.SemaphoreType.DMA((NY,)),
+        ],
+        compiler_params=pltpu.CompilerParams(collective_id=2, has_side_effects=True, vmem_limit_bytes=48 << 20),
+    )(omega, grads)
 
 
 def gram_kernel(part_ref, panel_ref, blocks_ref, rs_buf, mine, core_buf, chip, z_buf, strip, x_buf, sems):
@@ -161,30 +245,53 @@
 def eliminate(tiles):
     lane = lax.broadcasted_iota(jnp.int32, (8, B), 1)
     sub = lax.broadcasted_iota(jnp.int32, (8, B), 0)
-    for j in range(B):
-        first, at = divmod(j, 8)
+    count = B // 8
+
+    def spread(tile, k):
+        return jnp.broadcast_to(tile[k : k + 1, :], (8, B))
+
+    def columns(tile, b):
+        return [jnp.broadcast_to(tile[:, 8 * b + k : 8 * b + k + 1], (8, B)) for k in range(8)]
+
+    found = [[None] * count for _ in tiles]
+    for b in range(count):
+        inside = (lane >= 8 * b) & (lane < 8 * b + 8)
+        unit = (lane == sub + 8 * b).astype(F32)
+        states = []
         for rows in tiles:
-            row = rows[first][at : at + 1, :]
-            inverse = 1.0 / row[:, j : j + 1]
-            scaled = jnp.where(lane == j, 1.0, jnp.broadcast_to(row, (8, B))) * inverse
-            for t in range(first, B // 8):
-                if t == first and at == 7:
-                    continue
-                column = jnp.broadcast_to(rows[t][:, j : j + 1], (8, B))
-                new = jnp.where(lane == j, 0.0, rows[t]) - column * scaled
-                rows[t] = jnp.where(sub > at, new, rows[t]) if t == first else new
-    return tiles
+            start = jnp.where(inside, unit, rows[b])
+            states.append([columns(rows[b], b), start, start, jnp.zeros((8, B), F32)])
+        for k in range(8):
+            for state in states:
+                cols, jordan, forward, scale = state
+                pivot = spread(cols[k], k)
+                inverse = 1.0 / pivot
+                factor = cols[k] * inverse
+                for j in range(k + 1, 8):
+                    line = spread(cols[j], k)
+                    cols[j] = jnp.where(sub == k, line * inverse, cols[j] - factor * line)
+                line = spread(jordan, k)
+                state[1] = jnp.where(sub == k, line * inverse, jordan - factor * line)
+                state[2] = jnp.where(sub > k, forward - factor * spread(forward, k), forward)
+                state[3] = jnp.where(sub == k, pivot, scale)
+        for n, rows in enumerate(tiles):
+            cols, jordan, forward, scale = states[n]
+            found[n][b] = jnp.where(lane < 8 * b + 8, forward, 0.0) * lax.rsqrt(scale)
+            lines = [spread(jordan, k) for k in range(8)]
+            for t in range(b + 1, count):
+                cols = columns(rows[t], b)
+                terms = [cols[k] * lines[k] for k in range(8)]
+                while len(terms) > 1:
+                    terms = [terms[i] + terms[i + 1] for i in range(0, len(terms), 2)]
+                rows[t] = jnp.where(inside, 0.0, rows[t]) - terms[0]
+    return found
 
 
 def finish(rows):
-    whole = jnp.concatenate(rows, axis=0)
-    r = lax.broadcasted_iota(jnp.int32, (B, B), 0)
-    q = lax.broadcasted_iota(jnp.int32, (B, B), 1)
-    pivot = jnp.sum(jnp.where(r == q, whole, 0.0), axis=1, keepdims=True)
-    return jnp.where(q < r, whole, jnp.where(q == r, 1.0, 0.0)) * lax.rsqrt(pivot)
-
-
-def factor_kernel(blocks_ref, panel_ref, basis_ref, w):
+    return jnp.concatenate(rows, axis=0)
+
+
+def factor_kernel(blocks_ref, panel_ref, basis_ref, w, inv):
     for i in range(4):
         for j in range(i + 1):
             for layer, (who, at) in enumerate(((i, j), (3 - i, 4 - i + j))):
@@ -203,19 +310,38 @@
         inside = (q >= k * B) & (q < k * B + B)
         below = r >= k * B + B
         for n in range(LAYERS):
-            inverse = finish(tiles[n])
-            top = jnp.where(inside, eye.astype(F32), w[n, here, :])
-            right = jnp.dot(inverse, top, precision=HIGHEST, preferred_element_type=F32)
-            left = lax.dot_general(w[n, :, here], inverse, NT, precision=HIGHEST, preferred_element_type=F32)
-            left = jnp.where(below, left, 0.0)
-            rest = jnp.where(inside & below, 0.0, w[n])
-            w[n] = rest - jnp.dot(left, right, precision=HIGHEST, preferred_element_type=F32)
-            w[n, here, :] = jnp.where(q < k * B + B, right, 0.0)
+            inv[n] = finish(tiles[n])
+        for at in range(4):
+
+            @pl.when(k == at)
+            def _():
+                a, z = at * B, at * B + B
+                for n in range(LAYERS):
+                    inverse = inv[n]
+                    right = jnp.dot(inverse, w[n, a:z, :], precision=HIGHEST, preferred_element_type=F32)
+                    pieces = [right[:, :a], inverse, right[:, z:]]
+                    right = jnp.concatenate([p for p in pieces if p.shape[1]], axis=1)
+                    if z < RANK:
+                        left = lax.dot_general(
+                            w[n, z:, a:z], inverse, NT, precision=HIGHEST, preferred_element_type=F32
+                        )
+                        w[n, z:, a:z] = jnp.zeros((RANK - z, B), F32)
+                        w[n, z:, :] = w[n, z:, :] - jnp.dot(
+                            left, right, precision=HIGHEST, preferred_element_type=F32
+                        )
+                        right = jnp.concatenate([right[:, :z], jnp.zeros((B, RANK - z), F32)], axis=1)
+                    w[n, a:z, :] = right
+
         return carry
 
     lax.fori_loop(0, 4, step, 0)
     for n in range(LAYERS):
-        basis = lax.dot_general(panel_ref[n].astype(F32), w[n], NT, precision=HIGHEST, preferred_element_type=F32)
+        rest = w[n]
+        basis = jnp.zeros((ROWS, RANK), F32)
+        for _ in range(3):
+            part = rest.astype(BF)
+            rest = rest - part.astype(F32)
+            basis = basis + lax.dot_general(panel_ref[n], part, NT, preferred_element_type=F32)
         basis_ref[n] = basis.astype(BF)
 
 
@@ -226,7 +352,7 @@
         out_shape=jax.ShapeDtypeStruct((LAYERS, ROWS, RANK), BF),
         in_specs=[vmem, vmem],
         out_specs=vmem,
-        scratch_shapes=[pltpu.VMEM((LAYERS, RANK, RANK), F32)],
+        scratch_shapes=[pltpu.VMEM((LAYERS, RANK, RANK), F32), pltpu.VMEM((LAYERS, B, B), F32)],
         compiler_params=pltpu.CompilerParams(vmem_limit_bytes=32 << 20),
     )(blocks, panel)
 
@@ -388,8 +514,9 @@
 
 
 def local(grad_parts, omega, first_moment, second_moment):
-    summed = lax.psum_scatter(grad_parts[0], "dp", scatter_dimension=2, tiled=True)
-    part = jnp.einsum("lrd,dk->lrk", summed, omega, preferred_element_type=F32).astype(BF)
+    part = panel_part(omega, grad_parts[0])
+    grads, part = lax.optimization_barrier((grad_parts[0], part))
+    summed = lax.psum_scatter(grads, "dp", scatter_dimension=2, tiled=True)
     panel, blocks = gram(part)
     basis = factor(blocks, panel)
     return tail(basis, summed, first_moment, second_moment)

time: 332 us -> 249 us (0.75)
  waiting for transfers between devices: 90.4 us -> 0.76 us
  Pallas kernels: 221 us -> 228 us
    reduce_scatter x1, waiting for transfers between devices: 89.7 us -> 0.75 us  [local(): summed = lax.psum_scatter(grads, 'dp', scatter_dimension=2, tiled=True)]
    pallas_call x1, Pallas kernels: 84.2 us -> 28.9 us  [factor(): pl.pallas_call(factor_kernel, out_shape=jax.ShapeDtypeStruct((LAYERS, ROW...]
    pallas_call x0 -> x1, Pallas kernels: none -> 43.3 us  [panel_part(): pl.pallas_call(panel_kernel, out_shape=jax.ShapeDtypeStruct((LAYERS, ROWS...]
    pallas_call x1, Pallas kernels: 52.3 us -> 67.1 us  [gram(): pl.pallas_call(gram_kernel, out_shape=(jax.ShapeDtypeStruct((LAYERS, ROWS...]
    pallas_call x1, Pallas kernels: 84.3 us -> 88.6 us  [tail(): pl.pallas_call(tail_kernel, out_shape=(jax.ShapeDtypeStruct((8, LAYERS, O...]
  transfers between devices with their start and end apart: 1 -> 1, of which waited for: 1 -> 1; matrix products, arithmetic and copies ran while one was open for 0% -> 0% of each run, Pallas kernels for 0% -> 39%
where the time goes in v2:
time: 249 us
  Pallas kernels  228 us (92%)
  between operations  14.1 us (6%)
  local copies, waits for them, and re-layouts  5.82 us (2%)
    pallas_call x1, Pallas kernels, tail(): pl.pallas_call(tail_kernel, out_shape=(jax.ShapeDtypeStruct((8, LAYERS, O...  88.6 us
    pallas_call x1, Pallas kernels, gram(): pl.pallas_call(gram_kernel, out_shape=(jax.ShapeDtypeStruct((LAYERS, ROWS...  67.1 us
    pallas_call x1, Pallas kernels, panel_part(): pl.pallas_call(panel_kernel, out_shape=jax.ShapeDtypeStruct((LAYERS, ROWS...  43.3 us
    pallas_call x1, Pallas kernels, factor(): pl.pallas_call(factor_kernel, out_shape=jax.ShapeDtypeStruct((LAYERS, ROW...  28.9 us
    unnamed x11, local copies, waits for them, and re-layouts  5.82 us
  transfers between devices with their start and end apart: 1, of which 1 were waited for; matrix products, arithmetic and copies ran while one was open for 0% of the time, Pallas kernels for 39%

profile of v2, /device:TPU:1, one launch (start us, length us, event | category | flops | bytes accessed | tf_op | source)
XLA Modules:
  0.0 248.5 jit_solution(10343500877071867277)
XLA Ops:
  7.2 0.0 reduce-scatter.2.cloned.1.call-start
  7.2 0.0 copy-start.1
  7.2 1.6 copy-done.1
  8.8 43.3 %shard_map.67.part_ref = bf16[2,256,512]{2,1,0:T(8,128)(2,1)S(1)} custom-call(bf16[2048,512]{1,0:T(8,128)(2,1)S(1)} %copy-done.1, bf16[2,256,8192]{2,1,0:T(8,128)(2,1)} %bitcast.1), custom_call_target="tpu_custom_call" | custom-call | tf_op jit(solution)/shard_map/pallas_call | solution.py:134
  52.1 0.0 reduce-scatter.2.cloned.1.call-update
  52.1 0.0 copy-start.2
  52.1 0.0 copy-start.3
  52.1 67.1 %shard_map.68 = (bf16[2,256,512]{2,1,0:T(8,128)(2,1)S(1)}, f32[4,640,128]{2,1,0:T(8,128)S(1)}) custom-call(bf16[2,256,512]{2,1,0:T(8,128)(2,1)S(1)} %shard_map.67.part_ref), custom_call_target="tpu_custom_call" | custom-call | tf_op jit(solution)/shard_map/pallas_call | solution.py:223
  119.2 28.9 %shard_map.69.basis_ref = bf16[2,256,512]{2,1,0:T(8,128)(2,1)S(1)} custom-call(f32[4,640,128]{2,1,0:T(8,128)S(1)} %get-tuple-element.8.blocks_ref, bf16[2,256,512]{2,1,0:T(8,128)(2,1)S(1)} %get-tuple-element.9.panel_ref), custom_call_target="tpu_custom_call" | custom-call | tf_op jit(solution)/shard_map/pallas_call | solution.py:350
  148.1 0.7 reduce-scatter.2.cloned.1.call-done.summed_ref
  148.8 0.0 copy-done.2
  148.8 0.0 copy-done.3
  148.8 0.0 copy-start
  148.8 1.6 copy-done
  150.4 88.6 %shard_map.70 = (f32[8,2,2048]{2,1,0:T(2,128)S(1)}, f32[8,2,2048]{2,1,0:T(2,128)S(1)}, bf16[2,256,2048]{2,1,0:T(8,128)(2,1)S(1)}) custom-call(bf16[2,256,512]{2,1,0:T(8,128)(2,1)S(1)} %shard_map.69.basis_ref, bf16[2,256,2048]{2,1,0:T(8,128)(2,1)S(1)} %copy-done, f32[8,2,2048]{2,1,0:T(2,128)S(1)} %copy-done.2, f32[8,2,2048]{2,1,0:T(2,128)S(1)} %copy-done.3), custom_call_target="tpu_custom_call" | custom-call | tf_op jit(solution)/shard_map/pallas_call | solution.py:488
  239.0 0.7 copy.10
  239.7 0.7 copy.11
  240.3 1.3 copy.12
Async XLA Ops:
  7.2 141.6 %reduce-scatter.2.cloned.1.call-start = ((), (), s32[]{:S(2)}) async-start(), calls=%async_computation.1 | async-start | bytes 10485760 | tf_op jit(solution)/shard_map/reduce_scatter | solution.py:519
  7.2 1.6 copy-start.1
  52.1 96.7 %copy-start.2 = (f32[8,2,2048]{2,1,0:T(2,128)S(1)}, f32[8,2,2048]{2,1,0:T(2,128)}, u32[]{:S(2)}) copy-start(f32[8,2,2048]{2,1,0:T(2,128)} %first_ref.1) | copy-start | bytes 393220
  52.1 96.7 %copy-start.3 = (f32[8,2,2048]{2,1,0:T(2,128)S(1)}, f32[8,2,2048]{2,1,0:T(2,128)}, u32[]{:S(2)}) copy-start(f32[8,2,2048]{2,1,0:T(2,128)} %second_ref.1) | copy-start | bytes 393220
  148.8 1.6 copy-start
Sparse Core Ops, SparseCore 0:
  52.2 96.5 reduce-scatter.1

commit v3 on v2

--- a/solution.py
+++ b/solution.py
@@ -147,14 +147,22 @@
     )(omega, grads)
 
 
-def gram_kernel(part_ref, panel_ref, blocks_ref, rs_buf, mine, core_buf, chip, z_buf, strip, x_buf, sems):
+STREAMS = ((0, 1024), (1024, 1536))
+BLOCKS = LAYERS * 10 * B
+
+
+def rows_at(start, size):
+    return pl.ds(pl.multiple_of(start, 8), size)
+
+
+def gram_kernel(part_ref, panel_ref, blocks_ref, rs_buf, mine, core_buf, chip, x_buf, x_sum, z_buf, strip, y_buf, sems):
     spot = place()
     y, x, z, c = spot
-    peers = [along("y", spot, k) for k in range(1, NY)]
-    peers += [along("z", spot, k) for k in range(1, NZ)]
-    peers += [along("x", spot, k) for k in range(1, NX)]
-    peers += [along("c", spot, 1)]
-    greet(peers)
+    twin = along("c", spot, 1)
+    near_y = [along("y", spot, k) for k in range(1, NY)]
+    near_x = [along("x", spot, k) for k in range(1, NX)]
+    near_z = [along("z", spot, k) for k in range(1, NZ)]
+    greet([twin] + near_y + near_x + near_z)
     done = []
     count = [0]
 
@@ -164,56 +172,108 @@
         done.append(copy)
         return copy
 
+    def landed(copies):
+        for copy in copies:
+            copy.wait_recv()
+
     q = ROWS // NY
     own = span(y * q, q)
-    copies = [
-        go(part_ref.at[:, span(((y + k) % NY) * q, q), :], rs_buf.at[k - 1], along("y", spot, k)) for k in range(1, NY)
+    first = [
+        [
+            go(part_ref.at[n, span(((y + k) % NY) * q, q), :], rs_buf.at[k - 1, n], near_y[k - 1])
+            for k in range(1, NY)
+        ]
+        for n in range(LAYERS)
     ]
-    total = part_ref[:, own, :].astype(F32)
-    for k, copy in enumerate(copies):
-        copy.wait_recv()
-        total = total + rs_buf[k].astype(F32)
-    panel_ref[:, own, :] = total.astype(BF)
-    copies = [go(panel_ref.at[:, own, :], panel_ref.at[:, own, :], along("y", spot, k)) for k in range(1, NY)]
-    for copy in copies:
-        copy.wait_recv()
-
-    for b in range(5):
-        low = (y - b + 4) // 4
-        layer = 1 - low
-        i = low * y + (1 - low) * (3 - y)
-        j = low * b + (1 - low) * (b - y - 1)
-        left = panel_ref[layer, :, span(i * B, B)]
-        right = panel_ref[layer, :, span(j * B, B)]
-        mine[b * B : b * B + B, :] = lax.dot_general(left, right, TN, preferred_element_type=F32)
-
-    copy = go(mine.at[span((1 - c) * 320, 320), :], core_buf, along("c", spot, 1))
-    copy.wait_recv()
-    chip[...] = mine[span(c * 320, 320), :] + core_buf[...]
-    copies = [
-        go(chip.at[span(((z + k) % NZ) * 40, 40), :], z_buf.at[k - 1], along("z", spot, k)) for k in range(1, NZ)
-    ]
-    total = chip[span(z * 40, 40), :]
-    for k, copy in enumerate(copies):
-        copy.wait_recv()
-        total = total + z_buf[k]
-    strip[...] = total
-    copies = [go(strip, x_buf.at[k - 1], along("x", spot, k)) for k in range(1, NX)]
-    for k, copy in enumerate(copies):
-        copy.wait_recv()
-        total = total + x_buf[k]
-    place_of = pl.ds(pl.multiple_of(c * 320 + z * 40, 8), 40)
-    blocks_ref[y, place_of, :] = total
-    piece = blocks_ref.at[y, place_of, :]
-    copies = [go(piece, piece, along("z", spot, k)) for k in range(1, NZ)]
-    for copy in copies:
-        copy.wait_recv()
-    piece = blocks_ref.at[y, span(c * 320, 320), :]
-    copies = [go(piece, piece, along("y", spot, k)) for k in range(1, NY)]
-    for copy in copies:
-        copy.wait_recv()
-    piece = blocks_ref.at[:, span(c * 320, 320), :]
-    go(piece, piece, along("c", spot, 1)).wait_recv()
+    spread = []
+    for n in range(LAYERS):
+        landed(first[n])
+        total = part_ref[n, own, :].astype(F32)
+        for k in range(1, NY):
+            total = total + rs_buf[k - 1, n].astype(F32)
+        panel_ref[n, own, :] = total.astype(BF)
+        whole = panel_ref[n, own, :]
+        row = n * 10 * B
+        for i in range(4):
+            wide = (i + 1) * B
+            out = lax.dot_general(whole[:, i * B : wide], whole[:, :wide], TN, preferred_element_type=F32)
+            for j in range(i + 1):
+                mine[row : row + B, :] = out[:, j * B : j * B + B]
+                row += B
+        if n == 0:
+            start, size = STREAMS[0]
+            half = size // 2
+            flight = [
+                [go(mine.at[rows_at(start + (1 - c) * half, half), :], core_buf.at[pl.ds(start // 2, half), :], twin)]
+            ]
+    start, size = STREAMS[1]
+    half = size // 2
+    flight.append(
+        [go(mine.at[rows_at(start + (1 - c) * half, half), :], core_buf.at[pl.ds(start // 2, half), :], twin)]
+    )
+
+    for s, (start, size) in enumerate(STREAMS):
+        half, quarter = size // 2, size // 8
+        landed(flight[s])
+        here = pl.ds(start // 2, half)
+        chip[here, :] = mine[rows_at(start + c * half, half), :] + core_buf[here, :]
+        flight[s] = [
+            go(
+                chip.at[rows_at(start // 2 + ((x + k) % NX) * quarter, quarter), :],
+                x_buf.at[k - 1, pl.ds(start // 8, quarter), :],
+                near_x[k - 1],
+            )
+            for k in range(1, NX)
+        ]
+    for k in range(1, NY):
+        spread.append(go(panel_ref.at[:, own, :], panel_ref.at[:, own, :], near_y[k - 1]))
+    for s, (start, size) in enumerate(STREAMS):
+        quarter, piece = size // 8, size // 64
+        landed(flight[s])
+        total = chip[rows_at(start // 2 + x * quarter, quarter), :]
+        for k in range(1, NX):
+            total = total + x_buf[k - 1, start // 8 : start // 8 + quarter, :]
+        x_sum[start // 8 : start // 8 + quarter, :] = total
+        flight[s] = [
+            go(
+                x_sum.at[rows_at(start // 8 + ((z + k) % NZ) * piece, piece), :],
+                z_buf.at[k - 1, pl.ds(start // 64, piece), :],
+                near_z[k - 1],
+            )
+            for k in range(1, NZ)
+        ]
+    for s, (start, size) in enumerate(STREAMS):
+        piece = size // 64
+        landed(flight[s])
+        here = pl.ds(start // 64, piece)
+        total = x_sum[rows_at(start // 8 + z * piece, piece), :]
+        for k in range(1, NZ):
+            total = total + z_buf[k - 1, here, :]
+        strip[here, :] = total
+        flight[s] = [go(strip.at[here, :], y_buf.at[k - 1, here, :], near_y[k - 1]) for k in range(1, NY)]
+    for s, (start, size) in enumerate(STREAMS):
+        half, quarter, piece = size // 2, size // 8, size // 64
+        landed(flight[s])
+        here = pl.ds(start // 64, piece)
+        total = strip[here, :]
+        for k in range(1, NY):
+            total = total + y_buf[k - 1, here, :]
+        at = rows_at(start + c * half + x * quarter + z * piece, piece)
+        blocks_ref[at, :] = total
+        flight[s] = [go(blocks_ref.at[at, :], blocks_ref.at[at, :], peer) for peer in near_z]
+    for s, (start, size) in enumerate(STREAMS):
+        half, quarter = size // 2, size // 8
+        landed(flight[s])
+        at = rows_at(start + c * half + x * quarter, quarter)
+        flight[s] = [go(blocks_ref.at[at, :], blocks_ref.at[at, :], peer) for peer in near_x]
+    for s, (start, size) in enumerate(STREAMS):
+        half = size // 2
+        landed(flight[s])
+        at = rows_at(start + c * half, half)
+        flight[s] = [go(blocks_ref.at[at, :], blocks_ref.at[at, :], twin)]
+    for copies in flight:
+        landed(copies)
+    landed(spread)
     for copy in done:
         copy.wait_send()
 
@@ -224,19 +284,21 @@
         gram_kernel,
         out_shape=(
             jax.ShapeDtypeStruct((LAYERS, ROWS, RANK), BF),
-            jax.ShapeDtypeStruct((4, 640, B), F32),
+            jax.ShapeDtypeStruct((BLOCKS, B), F32),
         ),
         in_specs=[vmem],
         out_specs=(vmem, vmem),
         scratch_shapes=[
             pltpu.VMEM((NY - 1, LAYERS, ROWS // NY, RANK), BF),
-            pltpu.VMEM((640, B), F32),
-            pltpu.VMEM((320, B), F32),
-            pltpu.VMEM((320, B), F32),
-            pltpu.VMEM((NZ - 1, 40, B), F32),
-            pltpu.VMEM((40, B), F32),
-            pltpu.VMEM((NX - 1, 40, B), F32),
-            pltpu.SemaphoreType.DMA((2, 32)),
+            pltpu.VMEM((BLOCKS, B), F32),
+            pltpu.VMEM((BLOCKS // 2, B), F32),
+            pltpu.VMEM((BLOCKS // 2, B), F32),
+            pltpu.VMEM((NX - 1, BLOCKS // 8, B), F32),
+            pltpu.VMEM((BLOCKS // 8, B), F32),
+            pltpu.VMEM((NZ - 1, BLOCKS // 64, B), F32),
+            pltpu.VMEM((BLOCKS // 64, B), F32),
+            pltpu.VMEM((NY - 1, BLOCKS // 64, B), F32),
+            pltpu.SemaphoreType.DMA((2, 64)),
         ],
         compiler_params=pltpu.CompilerParams(collective_id=0, has_side_effects=True, vmem_limit_bytes=32 << 20),
     )(part)
@@ -292,13 +354,15 @@
 
 
 def factor_kernel(blocks_ref, panel_ref, basis_ref, w, inv):
-    for i in range(4):
-        for j in range(i + 1):
-            for layer, (who, at) in enumerate(((i, j), (3 - i, 4 - i + j))):
-                block = blocks_ref[who, at * B : at * B + B, :]
-                w[layer, i * B : i * B + B, j * B : j * B + B] = block
+    for n in range(LAYERS):
+        row = n * 10 * B
+        for i in range(4):
+            for j in range(i + 1):
+                block = blocks_ref[row : row + B, :]
+                row += B
+                w[n, i * B : i * B + B, j * B : j * B + B] = block
                 if i != j:
-                    w[layer, j * B : j * B + B, i * B : i * B + B] = block.T
+                    w[n, j * B : j * B + B, i * B : i * B + B] = block.T
 
     def step(k, carry):
         here = span(k * B, B)
@@ -365,26 +429,38 @@
     new_first_ref,
     new_second_ref,
     delta_ref,
+    summed,
     twin_basis,
     twin_summed,
-    x_out,
-    x_in,
+    twin_first,
+    twin_second,
+    back_first,
+    back_second,
+    relay_out,
+    relay_in,
+    near_out,
+    near_in,
     x_own,
     z_out,
     z_in,
     z_own,
-    full,
-    fresh,
     joined,
     gathered,
     sems,
+    local_sems,
 ):
     spot = place()
     y, x, z, c = spot
-    peers = [along("c", spot, 1)]
-    peers += [along("x", spot, k) for k in range(1, NX)]
-    peers += [along("z", spot, k) for k in range(1, NZ)]
-    greet(peers)
+    twin = along("c", spot, 1)
+    up, down = along("x", spot, 1), along("x", spot, NX - 1)
+    near_z = [along("z", spot, k) for k in range(1, NZ)]
+    mine, other = span(c * HALF, HALF), span((1 - c) * HALF, HALF)
+    loads = []
+    for n in range(LAYERS):
+        load = pltpu.make_async_copy(summed_ref.at[n, :, mine], summed.at[n], local_sems.at[n])
+        load.start()
+        loads.append(load)
+    greet([twin, up, down] + near_z)
     done = []
     count = [0]
 
@@ -394,91 +470,131 @@
         done.append(copy)
         return copy
 
-    mine, other = span(c * HALF, HALF), span((1 - c) * HALF, HALF)
-    twin = along("c", spot, 1)
+    def landed(copies):
+        for copy in copies:
+            copy.wait_recv()
+
     got = [
-        (go(basis_ref.at[n], twin_basis.at[n], twin), go(summed_ref.at[n, :, other], twin_summed.at[n], twin))
+        [go(basis_ref.at[n], twin_basis.at[n], twin), go(summed_ref.at[n, :, other], twin_summed.at[n], twin)]
         for n in range(LAYERS)
     ]
-
-    def product(n, part):
-        here = span(part * B, B)
-        out = lax.dot_general(basis_ref[n, :, here], summed_ref[n, :, mine], TN, preferred_element_type=F32)
+    moments = [
+        go(first_ref.at[:, :, other], twin_first, twin),
+        go(second_ref.at[:, :, other], twin_second, twin),
+    ]
+
+    def product(n, start, size):
+        here = span(start, size)
+        out = lax.dot_general(basis_ref[n, :, here], summed[n], TN, preferred_element_type=F32)
         return out + lax.dot_general(twin_basis[n, :, here], twin_summed[n], TN, preferred_element_type=F32)
 
-    x_copies = []
-    for n in range(LAYERS):
-        for copy in got[n]:
-            copy.wait_recv()
-        copies = []
-        for k in (2, 1, 3):
-            x_out[n, k - 1] = product(n, (x + k) % NX).astype(BF)
-            copies.append((k, go(x_out.at[n, k - 1], x_in.at[n, k - 1], along("x", spot, k))))
-        x_own[n] = product(n, x)
-        x_copies.append(copies)
+    h = B // 2
+    above, below, across = ((x + 1) % NX) * B, ((x + NX - 1) % NX) * B, ((x + 2) % NX) * B
+    relays, nears = [], []
+    for n in range(LAYERS):
+        landed(got[n])
+        loads[n].wait()
+        far = product(n, across, B)
+        relay_out[n, 0] = far[:h].astype(BF)
+        relay_out[n, 1] = far[h:].astype(BF)
+        relays.append([go(relay_out.at[n, 0], relay_in.at[n, 0], up), go(relay_out.at[n, 1], relay_in.at[n, 1], down)])
+        x_own[n, 1] = product(n, above, B)
+        near_out[n, 0, h:, :] = x_own[n, 1, h:, :].astype(BF)
+        copies = [go(near_out.at[n, 0, pl.ds(h, h), :], near_in.at[n, 0, pl.ds(h, h), :], up)]
+        x_own[n, 2] = product(n, below, B)
+        near_out[n, 1, :h, :] = x_own[n, 2, :h, :].astype(BF)
+        copies.append(go(near_out.at[n, 1, pl.ds(0, h), :], near_in.at[n, 1, pl.ds(0, h), :], down))
+        nears.append(copies)
+        x_own[n, 0] = product(n, x * B, B)
+    for n in range(LAYERS):
+        relays[n][0].wait_recv()
+        near_out[n, 0, :h, :] = (x_own[n, 1, :h, :] + relay_in[n, 0].astype(F32)).astype(BF)
+        nears[n].append(go(near_out.at[n, 0, pl.ds(0, h), :], near_in.at[n, 0, pl.ds(0, h), :], up))
+        relays[n][1].wait_recv()
+        near_out[n, 1, h:, :] = (x_own[n, 2, h:, :] + relay_in[n, 1].astype(F32)).astype(BF)
+        nears[n].append(go(near_out.at[n, 1, pl.ds(h, h), :], near_in.at[n, 1, pl.ds(h, h), :], down))
 
     z_copies = []
     for n in range(LAYERS):
-        for k, copy in x_copies[n]:
-            copy.wait_recv()
-        total = x_own[n]
-        for k in range(1, NX):
-            total = total + x_in[n, k - 1].astype(F32)
-        x_own[n] = total
+        landed(nears[n])
+        total = x_own[n, 0] + near_in[n, 0].astype(F32) + near_in[n, 1].astype(F32)
+        x_own[n, 0] = total
         z_out[n] = total.astype(BF)
-        z_own[n] = x_own[n, span(z * 16, 16), :]
         z_copies.append(
-            [go(z_out.at[n, span(((z + k) % NZ) * 16, 16), :], z_in.at[n, k - 1], along("z", spot, k)) for k in range(1, NZ)]
+            [go(z_out.at[n, span(((z + k) % NZ) * 16, 16), :], z_in.at[n, k - 1], near_z[k - 1]) for k in range(1, NZ)]
         )
-    for n in range(LAYERS):
-        total = z_own[n]
-        for k, copy in enumerate(z_copies[n]):
-            copy.wait_recv()
-            total = total + z_in[n, k].astype(F32)
+    landed(moments)
+    slot = span(x * B + z * 16, 16)
+    ours, theirs = span(c * 8, 8), span((1 - c) * 8, 8)
+    spreads = []
+    for n in range(LAYERS):
+        landed(z_copies[n])
+        total = x_own[n, 0, span(z * 16, 16), :]
+        for k in range(1, NZ):
+            total = total + z_in[n, k - 1].astype(F32)
         z_own[n] = total
 
-    copy = go(z_own.at[:, span((1 - c) * 8, 8), :], full.at[:, :, mine], twin)
-    full[:, :, mine] = z_own[:, span(c * 8, 8), :]
-    copy.wait_recv()
-    for n in range(LAYERS):
-        projected = full[n]
-        new_first = 0.9 * first_ref[:, n, :] + 0.1 * projected
-        new_second = 0.999 * second_ref[:, n, :] + 0.001 * projected * projected
-        new_first_ref[:, n, :] = new_first
-        new_second_ref[:, n, :] = new_second
-        fresh[n] = new_first / (jnp.sqrt(new_second) + 1e-08)
-    rows = span(c * 8, 8)
-    copy = go(fresh.at[:, :, other], joined.at[:, rows, :], twin)
-    joined[:, rows, :] = fresh[:, :, mine]
-    copy.wait_recv()
-
-    slot = span(x * B + z * 16, 16)
-    gathered[c, :, slot, :] = joined[...].astype(BF)
-    piece = gathered.at[c, :, slot, :]
-    copies = [go(piece, piece, along("z", spot, k)) for k in range(1, NZ)]
-    for copy in copies:
-        copy.wait_recv()
-    piece = gathered.at[c, :, span(x * B, B), :]
-    copies = [(k, go(piece, piece, along("x", spot, k))) for k in (2, 1, 3)]
-    crossed = [go(piece, piece, twin)]
-    for k, copy in copies[1:] + copies[:1]:
-        copy.wait_recv()
-        piece = gathered.at[c, :, span(((x - k + NX) % NX) * B, B), :]
-        crossed.append(go(piece, piece, twin))
-    for copy in crossed:
-        copy.wait_recv()
-
+        def adam(projected, first, second):
+            new_first = 0.9 * first + 0.1 * projected
+            new_second = 0.999 * second + 0.001 * projected * projected
+            return new_first, new_second, new_first / (jnp.sqrt(new_second) + 1e-08)
+
+        new_first, new_second, fresh = adam(z_own[n, ours, :], first_ref[:, n, mine], second_ref[:, n, mine])
+        new_first_ref[:, n, mine] = new_first
+        new_second_ref[:, n, mine] = new_second
+        joined[n, ours, :] = fresh
+        new_first, new_second, fresh = adam(z_own[n, theirs, :], twin_first[:, n, :], twin_second[:, n, :])
+        back_first[:, n, :] = new_first
+        back_second[:, n, :] = new_second
+        joined[n, theirs, :] = fresh
+        gathered[c, n, slot, :] = joined[n].astype(BF)
+        piece = gathered.at[c, n, slot, :]
+        spreads.append([go(piece, piece, peer) for peer in near_z])
+    backs = [
+        go(back_first, new_first_ref.at[:, :, mine], twin),
+        go(back_second, new_second_ref.at[:, :, mine], twin),
+    ]
+
+    def part(n, start, size):
+        return gathered.at[c, n, pl.ds(pl.multiple_of(start, size), size), :]
+
+    firsts, crossed = [], []
+    for n in range(LAYERS):
+        landed(spreads[n])
+        low, high, whole = part(n, x * B, h), part(n, x * B + h, h), part(n, x * B, B)
+        firsts.append([go(low, low, up), go(high, high, down), go(high, high, up), go(low, low, down)])
+        crossed.append([go(whole, whole, twin)])
+    seconds = []
+    for n in range(LAYERS):
+        firsts[n][0].wait_recv()
+        low = part(n, below, h)
+        seconds.append([go(low, low, up)])
+        firsts[n][1].wait_recv()
+        high = part(n, above + h, h)
+        seconds[n].append(go(high, high, down))
+        landed(firsts[n][2:])
+        for start in (below, above):
+            whole = part(n, start, B)
+            crossed[n].append(go(whole, whole, twin))
     tile = 256
     for n in range(LAYERS):
-        for half in range(2):
-
+        landed(seconds[n])
+        whole = part(n, across, B)
+        crossed[n].append(go(whole, whole, twin))
+
+        def make(half):
             def body(t, carry):
                 right = gathered[half, n, :, span(t * tile, tile)]
                 out = jnp.dot(basis_ref[n], right, preferred_element_type=F32)
-                delta_ref[n, :, span(half * HALF + t * tile, tile)] = out.astype(BF)
+                delta_ref[n, :, pl.ds(pl.multiple_of(half * HALF + t * tile, tile), tile)] = out.astype(BF)
                 return carry
 
             lax.fori_loop(0, HALF // tile, body, 0)
+
+        make(c)
+        landed(crossed[n])
+        make(1 - c)
+    landed(backs)
     for copy in done:
         copy.wait_send()
 
@@ -492,22 +608,28 @@
             jax.ShapeDtypeStruct((8, LAYERS, OWN), F32),
             jax.ShapeDtypeStruct((LAYERS, ROWS, OWN), BF),
         ),
-        in_specs=[vmem] * 4,
+        in_specs=[vmem, pl.BlockSpec(memory_space=pl.ANY), vmem, vmem],
         out_specs=(vmem,) * 3,
         scratch_shapes=[
+            pltpu.VMEM((LAYERS, ROWS, HALF), BF),
             pltpu.VMEM((LAYERS, ROWS, RANK), BF),
             pltpu.VMEM((LAYERS, ROWS, HALF), BF),
-            pltpu.VMEM((LAYERS, NX - 1, B, HALF), BF),
-            pltpu.VMEM((LAYERS, NX - 1, B, HALF), BF),
-            pltpu.VMEM((LAYERS, B, HALF), F32),
+            pltpu.VMEM((8, LAYERS, HALF), F32),
+            pltpu.VMEM((8, LAYERS, HALF), F32),
+            pltpu.VMEM((8, LAYERS, HALF), F32),
+            pltpu.VMEM((8, LAYERS, HALF), F32),
+            pltpu.VMEM((LAYERS, 2, B // 2, HALF), BF),
+            pltpu.VMEM((LAYERS, 2, B // 2, HALF), BF),
+            pltpu.VMEM((LAYERS, 2, B, HALF), BF),
+            pltpu.VMEM((LAYERS, 2, B, HALF), BF),
+            pltpu.VMEM((LAYERS, 3, B, HALF), F32),
             pltpu.VMEM((LAYERS, B, HALF), BF),
             pltpu.VMEM((LAYERS, NZ - 1, 16, HALF), BF),
             pltpu.VMEM((LAYERS, 16, HALF), F32),
-            pltpu.VMEM((LAYERS, 8, OWN), F32),
-            pltpu.VMEM((LAYERS, 8, OWN), F32),
             pltpu.VMEM((LAYERS, 16, HALF), F32),
             pltpu.VMEM((2, LAYERS, RANK, HALF), BF),
-            pltpu.SemaphoreType.DMA((2, 48)),
+            pltpu.SemaphoreType.DMA((2, 80)),
+            pltpu.SemaphoreType.DMA((LAYERS,)),
         ],
         compiler_params=pltpu.CompilerParams(collective_id=1, has_side_effects=True, vmem_limit_bytes=48 << 20),
     )(basis, summed, first, second)

time: 249 us -> 222 us (0.89)
  Pallas kernels: 228 us -> 190 us
  waiting for transfers between devices: 0.76 us -> 11.9 us
    pallas_call x1, Pallas kernels: 88.6 us -> 67.7 us  [tail(): pl.pallas_call(tail_kernel, out_shape=(jax.ShapeDtypeStruct((8, LAYERS, O...]
    pallas_call x1, Pallas kernels: 67.1 us -> 50.1 us  [gram(): pl.pallas_call(gram_kernel, out_shape=(jax.ShapeDtypeStruct((LAYERS, ROWS...]
    reduce_scatter x1, waiting for transfers between devices: 0.75 us -> 11.9 us  [local(): summed = lax.psum_scatter(grads, 'dp', scatter_dimension=2, tiled=True)]
  transfers between devices with their start and end apart: 1 -> 1, of which waited for: 1 -> 1; matrix products, arithmetic and copies ran while one was open for 0% -> 0% of each run, Pallas kernels for 39% -> 36%
where the time goes in v3:
time: 222 us; the launch traced here: 221 us
  Pallas kernels  190 us (86%)
  between operations  14.1 us (6%)
  waiting for transfers between devices  11.9 us (5%)
  local copies, waits for them, and re-layouts  5.82 us (3%)
    pallas_call x1, Pallas kernels, tail(): pl.pallas_call(tail_kernel, out_shape=(jax.ShapeDtypeStruct((8, LAYERS, O...  67.7 us
    pallas_call x1, Pallas kernels, gram(): pl.pallas_call(gram_kernel, out_shape=(jax.ShapeDtypeStruct((LAYERS, ROWS...  50.1 us
    pallas_call x1, Pallas kernels, panel_part(): pl.pallas_call(panel_kernel, out_shape=jax.ShapeDtypeStruct((LAYERS, ROWS...  43.3 us
    pallas_call x1, Pallas kernels, factor(): pl.pallas_call(factor_kernel, out_shape=jax.ShapeDtypeStruct((LAYERS, ROW...  28.6 us
    reduce_scatter x1, waiting for transfers between devices, local(): summed = lax.psum_scatter(grads, 'dp', scatter_dimension=2, tiled=True)  11.9 us
    unnamed x11, local copies, waits for them, and re-layouts  5.82 us
  transfers between devices with their start and end apart: 1, of which 1 were waited for; matrix products, arithmetic and copies ran while one was open for 0% of the time, Pallas kernels for 36%

profile of v3, /device:TPU:1, one launch (start us, length us, event | category | flops | bytes accessed | tf_op | source)
XLA Modules:
  0.0 221.5 jit_solution(8557832612472143873)
XLA Ops:
  7.2 0.0 reduce-scatter.2.cloned.1.call-start
  7.2 0.0 copy-start.1
  7.2 1.6 copy-done.1
  8.8 43.3 %shard_map.67.part_ref = bf16[2,256,512]{2,1,0:T(8,128)(2,1)S(1)} custom-call(bf16[2048,512]{1,0:T(8,128)(2,1)S(1)} %copy-done.1, bf16[2,256,8192]{2,1,0:T(8,128)(2,1)} %bitcast.1), custom_call_target="tpu_custom_call" | custom-call | tf_op jit(solution)/shard_map/pallas_call | solution.py:134
  52.1 0.0 reduce-scatter.2.cloned.1.call-update
  52.1 0.0 copy-start.2
  52.1 0.0 copy-start.3
  52.1 50.1 %shard_map.68 = (bf16[2,256,512]{2,1,0:T(8,128)(2,1)S(1)}, f32[2560,128]{1,0:T(8,128)S(1)}) custom-call(bf16[2,256,512]{2,1,0:T(8,128)(2,1)S(1)} %shard_map.67.part_ref), custom_call_target="tpu_custom_call" | custom-call | tf_op jit(solution)/shard_map/pallas_call | solution.py:283
  102.2 28.6 %shard_map.69.basis_ref = bf16[2,256,512]{2,1,0:T(8,128)(2,1)S(1)} custom-call(f32[2560,128]{1,0:T(8,128)S(1)} %get-tuple-element.8.blocks_ref, bf16[2,256,512]{2,1,0:T(8,128)(2,1)S(1)} %get-tuple-element.9.panel_ref), custom_call_target="tpu_custom_call" | custom-call | tf_op jit(solution)/shard_map/pallas_call | solution.py:414
  130.8 11.9 %reduce-scatter.2.cloned.1.call-done.summed_ref = bf16[2,256,2048]{2,1,0:T(8,128)(2,1)} async-done(((bf16[2,256,8192]{2,1,0:T(8,128)(2,1)}), bf16[2,256,2048]{2,1,0:T(8,128)(2,1)}) %reduce-scatter.2.cloned.1.call-update) | async-done | bytes 2097168 | tf_op jit(solution)/shard_map/reduce_scatter | solution.py:641
  142.7 0.0 copy-done.2
  142.7 0.0 copy-done.3
  142.7 0.0 copy-start
  142.7 1.6 copy-done
  144.3 67.7 %shard_map.70 = (f32[8,2,2048]{2,1,0:T(2,128)S(1)}, f32[8,2,2048]{2,1,0:T(2,128)S(1)}, bf16[2,256,2048]{2,1,0:T(8,128)(2,1)S(1)}) custom-call(bf16[2,256,512]{2,1,0:T(8,128)(2,1)S(1)} %shard_map.69.basis_ref, bf16[2,256,2048]{2,1,0:T(8,128)(2,1)S(1)} %copy-done, f32[8,2,2048]{2,1,0:T(2,128)S(1)} %copy-done.2, f32[8,2,2048]{2,1,0:T(2,128)S(1)} %copy-done.3), custom_call_target="tpu_custom_call" | custom-call | tf_op jit(solution)/shard_map/pallas_call | solution.py:604
  212.0 0.7 copy.10
  212.6 0.7 copy.11
  213.3 1.3 copy.12
Async XLA Ops:
  7.2 135.5 %reduce-scatter.2.cloned.1.call-start = ((), (), s32[]{:S(2)}) async-start(), calls=%async_computation.1 | async-start | bytes 10485760 | tf_op jit(solution)/shard_map/reduce_scatter | solution.py:641
  7.2 1.6 copy-start.1
  52.1 90.6 %copy-start.2 = (f32[8,2,2048]{2,1,0:T(2,128)S(1)}, f32[8,2,2048]{2,1,0:T(2,128)}, u32[]{:S(2)}) copy-start(f32[8,2,2048]{2,1,0:T(2,128)} %first_ref.1) | copy-start | bytes 393220
  52.1 90.6 %copy-start.3 = (f32[8,2,2048]{2,1,0:T(2,128)S(1)}, f32[8,2,2048]{2,1,0:T(2,128)}, u32[]{:S(2)}) copy-start(f32[8,2,2048]{2,1,0:T(2,128)} %second_ref.1) | copy-start | bytes 393220
  142.7 1.6 copy-start
Sparse Core Ops, SparseCore 0:
  52.2 90.4 reduce-scatter.1

commit v4 on v3

--- a/solution.py
+++ b/solution.py
@@ -63,105 +63,54 @@
     return pl.ds(pl.multiple_of(start, size), size)
 
 
-def panel_kernel(omega_ref, grads_hbm, part_ref, grads, far, total, sems, local_sems):
-    spot = place()
-    y, x, z, c = spot
-    up, down, twin = along("y", spot, 1), along("y", spot, NY - 1), along("c", spot, 1)
-    order = (0, NY - 1, 1, 2)
-    loads = []
-    for k in order:
-        columns = span(((y + k) % NY) * OWN, OWN)
-        load = pltpu.make_async_copy(grads_hbm.at[:, :, columns], grads.at[k], local_sems.at[k])
-        load.start()
-        loads.append(load)
-    greet([up, down, twin])
-    done = []
-    count = [0]
-
-    def go(src, dst, peer):
-        copy = ship(src, dst, sems.at[0, count[0]], sems.at[1, count[0]], peer)
-        count[0] += 1
-        done.append(copy)
-        return copy
-
-    q = OWN // 4
-    rows = [span(c * 2 * q + h * q, q) for h in range(2)]
-    near = [None] * 4
-    near[0] = go(omega_ref.at[rows[0], :], far.at[0, rows[0], :], up)
-    near[1] = go(omega_ref.at[rows[1], :], far.at[1, rows[1], :], down)
-    near[2] = go(omega_ref.at[rows[1], :], far.at[0, rows[1], :], up)
-    near[3] = go(omega_ref.at[rows[0], :], far.at[1, rows[0], :], down)
-
-    def add(k, matrix, fresh):
-        for n in range(LAYERS):
-            out = jnp.dot(grads[k, n], matrix[...], preferred_element_type=F32)
-            total[n] = out if fresh else total[n] + out
-
-    loads[0].wait()
-    add(0, omega_ref, True)
-    near[0].wait_recv()
-    relay = [go(far.at[0, rows[0], :], far.at[2, rows[0], :], up)]
-    crossed = [go(far.at[0, rows[0], :], far.at[0, rows[0], :], twin)]
-    near[1].wait_recv()
-    relay.append(go(far.at[1, rows[1], :], far.at[2, rows[1], :], down))
-    crossed.append(go(far.at[1, rows[1], :], far.at[1, rows[1], :], twin))
-    near[2].wait_recv()
-    crossed.append(go(far.at[0, rows[1], :], far.at[0, rows[1], :], twin))
-    near[3].wait_recv()
-    crossed.append(go(far.at[1, rows[0], :], far.at[1, rows[0], :], twin))
-    crossed[0].wait_recv()
-    crossed[2].wait_recv()
-    loads[1].wait()
-    add(NY - 1, far.at[0], False)
-    crossed[1].wait_recv()
-    crossed[3].wait_recv()
-    loads[2].wait()
-    add(1, far.at[1], False)
-    for h, copy in enumerate(relay):
-        copy.wait_recv()
-        crossed.append(go(far.at[2, rows[h], :], far.at[2, rows[h], :], twin))
-    crossed[4].wait_recv()
-    crossed[5].wait_recv()
-    loads[3].wait()
-    add(2, far.at[2], False)
-    part_ref[...] = total[...].astype(BF)
-    for copy in done:
-        copy.wait_send()
-
-
-def panel_part(omega, grads):
-    vmem = pl.BlockSpec(memory_space=pltpu.VMEM)
-    return pl.pallas_call(
-        panel_kernel,
-        out_shape=jax.ShapeDtypeStruct((LAYERS, ROWS, RANK), BF),
-        in_specs=[vmem, pl.BlockSpec(memory_space=pl.ANY)],
-        out_specs=vmem,
-        scratch_shapes=[
-            pltpu.VMEM((NY, LAYERS, ROWS, OWN), BF),
-            pltpu.VMEM((NY - 1, OWN, RANK), BF),
-            pltpu.VMEM((LAYERS, ROWS, RANK), F32),
-            pltpu.SemaphoreType.DMA((2, 12)),
-            pltpu.SemaphoreType.DMA((NY,)),
-        ],
-        compiler_params=pltpu.CompilerParams(collective_id=2, has_side_effects=True, vmem_limit_bytes=48 << 20),
-    )(omega, grads)
-
-
 STREAMS = ((0, 1024), (1024, 1536))
 BLOCKS = LAYERS * 10 * B
+FAR = NY - 1
 
 
 def rows_at(start, size):
     return pl.ds(pl.multiple_of(start, 8), size)
 
 
-def gram_kernel(part_ref, panel_ref, blocks_ref, rs_buf, mine, core_buf, chip, x_buf, x_sum, z_buf, strip, y_buf, sems):
+def front_kernel(
+    omega_hbm,
+    grads_hbm,
+    summed_ref,
+    panel_ref,
+    blocks_ref,
+    omega_ref,
+    grads,
+    omegas,
+    relay_in,
+    joint,
+    near_in,
+    partial,
+    part,
+    rs_buf,
+    mine,
+    core_buf,
+    chip,
+    x_buf,
+    x_sum,
+    z_buf,
+    strip,
+    y_buf,
+    sems,
+    local_sems,
+):
     spot = place()
     y, x, z, c = spot
     twin = along("c", spot, 1)
     near_y = [along("y", spot, k) for k in range(1, NY)]
     near_x = [along("x", spot, k) for k in range(1, NX)]
     near_z = [along("z", spot, k) for k in range(1, NZ)]
+    loads = [pltpu.make_async_copy(omega_hbm, omega_ref, local_sems.at[NY])]
+    loads[0].start()
+    for k in (0, 1, 3, 2):
+        columns = span(((y + k) % NY) * OWN, OWN)
+        load = pltpu.make_async_copy(grads_hbm.at[:, :, columns], grads.at[k], local_sems.at[k])
+        load.start()
+        loads.append(load)
     greet([twin] + near_y + near_x + near_z)
     done = []
     count = [0]
@@ -176,11 +125,108 @@
         for copy in copies:
             copy.wait_recv()
 
+    relays, nears = [None] * 2, [None] * 2
+
+    def launch(part_of):
+        off = (1 - part_of) * HALF
+
+        def columns(k):
+            return span(((y + k) % NY) * OWN + off, HALF)
+
+        relays[part_of] = [
+            go(grads_hbm.at[0, :, columns(2)], relay_in.at[part_of, 0], near_y[0]),
+            go(grads_hbm.at[1, :, columns(2)], relay_in.at[part_of, 1], near_y[2]),
+        ]
+        nears[part_of] = [
+            go(grads_hbm.at[1, :, columns(1)], near_in.at[part_of, 0, 1], near_y[0]),
+            go(grads_hbm.at[0, :, columns(3)], near_in.at[part_of, 1, 0], near_y[2]),
+        ]
+
+    def in_rows(work):
+        def body(t, carry):
+            work(span(t * 32, 32))
+            return carry
+
+        lax.fori_loop(0, ROWS // 32, body, 0)
+
+    def combine(part_of):
+        off = (1 - part_of) * HALF
+        for n, k in ((0, 1), (1, 3)):
+            relays[part_of][n].wait_recv()
+
+            def work(at):
+                own_term = grads[k, n, at, off : off + HALF].astype(F32)
+                joint[part_of, n, at, :] = (own_term + relay_in[part_of, n, at, :].astype(F32)).astype(BF)
+
+            in_rows(work)
+            nears[part_of].append(go(joint.at[part_of, n], near_in.at[part_of, n, n], near_y[k - 1]))
+
+    def finish_sum(part_of):
+        off = (1 - part_of) * HALF
+        landed(nears[part_of])
+
+        def work(at):
+            for n in range(LAYERS):
+                out = grads[0, n, at, off : off + HALF].astype(F32) + near_in[part_of, 0, n, at, :].astype(F32)
+                summed_ref[n, at, off : off + HALF] = (out + near_in[part_of, 1, n, at, :].astype(F32)).astype(BF)
+
+        in_rows(work)
+
+    strip_at = span(x * 256 + c * B + z * 16, 16)
+    slices = [go(omega_hbm.at[strip_at, :], omegas.at[FAR - k, strip_at, :], near_y[k - 1]) for k in range(1, NY)]
+    launch(0)
+
+    def block(s, which, start, size):
+        return omegas.at[s, pl.ds(pl.multiple_of(which * 256 + c * B + start, size), size), :]
+
+    flights = []
+    for s in range(FAR):
+        slices[FAR - 1 - s].wait_recv()
+        piece = omegas.at[s, strip_at, :]
+        flights.append([go(piece, piece, peer) for peer in near_z])
+    for load in loads:
+        load.wait()
+    for n in range(LAYERS):
+        partial[n] = jnp.dot(grads[0, n, :, :HALF], omega_ref[:HALF, :], preferred_element_type=F32)
+    up, down = near_x[0], near_x[2]
+    above, below, across = (x + 1) % NX, (x + NX - 1) % NX, (x + 2) % NX
+    h = B // 2
+    firsts, crossed, seconds = [], [], []
+    for s in range(FAR):
+        landed(flights[s])
+        low, high, whole = block(s, x, 0, h), block(s, x, h, h), block(s, x, 0, B)
+        firsts.append([go(low, low, up), go(high, high, down), go(high, high, up), go(low, low, down)])
+        crossed.append([go(whole, whole, twin)])
+    combine(0)
+    for s in range(FAR):
+        firsts[s][0].wait_recv()
+        low = block(s, below, 0, h)
+        seconds.append([go(low, low, up)])
+        firsts[s][1].wait_recv()
+        high = block(s, above, h, h)
+        seconds[s].append(go(high, high, down))
+        landed(firsts[s][2:])
+        for which in (below, above):
+            whole = block(s, which, 0, B)
+            crossed[s].append(go(whole, whole, twin))
+    for s in range(FAR):
+        landed(seconds[s])
+        whole = block(s, across, 0, B)
+        crossed[s].append(go(whole, whole, twin))
+    for s in range(FAR):
+        landed(crossed[s])
+        for n in range(LAYERS):
+            partial[n] += jnp.dot(grads[s + 1, n, :, :HALF], omegas[s], preferred_element_type=F32)
+    finish_sum(0)
+    for n in range(LAYERS):
+        out = partial[n] + jnp.dot(summed_ref[n, :, HALF:], omega_ref[HALF:, :], preferred_element_type=F32)
+        part[n] = out.astype(BF)
+
     q = ROWS // NY
     own = span(y * q, q)
     first = [
         [
-            go(part_ref.at[n, span(((y + k) % NY) * q, q), :], rs_buf.at[k - 1, n], near_y[k - 1])
+            go(part.at[n, span(((y + k) % NY) * q, q), :], rs_buf.at[k - 1, n], near_y[k - 1])
             for k in range(1, NY)
         ]
         for n in range(LAYERS)
@@ -188,7 +234,9 @@
     spread = []
     for n in range(LAYERS):
         landed(first[n])
-        total = part_ref[n, own, :].astype(F32)
+        if n == 1:
+            launch(1)
+        total = part[n, own, :].astype(F32)
         for k in range(1, NY):
             total = total + rs_buf[k - 1, n].astype(F32)
         panel_ref[n, own, :] = total.astype(BF)
@@ -242,6 +290,7 @@
             )
             for k in range(1, NZ)
         ]
+    combine(1)
     for s, (start, size) in enumerate(STREAMS):
         piece = size // 64
         landed(flight[s])
@@ -271,6 +320,7 @@
         landed(flight[s])
         at = rows_at(start + c * half, half)
         flight[s] = [go(blocks_ref.at[at, :], blocks_ref.at[at, :], twin)]
+    finish_sum(1)
     for copies in flight:
         landed(copies)
     landed(spread)
@@ -278,17 +328,26 @@
         copy.wait_send()
 
 
-def gram(part):
+def front(omega, grads):
     vmem = pl.BlockSpec(memory_space=pltpu.VMEM)
     return pl.pallas_call(
-        gram_kernel,
+        front_kernel,
         out_shape=(
+            jax.ShapeDtypeStruct((LAYERS, ROWS, OWN), BF),
             jax.ShapeDtypeStruct((LAYERS, ROWS, RANK), BF),
             jax.ShapeDtypeStruct((BLOCKS, B), F32),
         ),
-        in_specs=[vmem],
-        out_specs=(vmem, vmem),
+        in_specs=[pl.BlockSpec(memory_space=pl.ANY)] * 2,
+        out_specs=(vmem, vmem, vmem),
         scratch_shapes=[
+            pltpu.VMEM((OWN, RANK), BF),
+            pltpu.VMEM((NY, LAYERS, ROWS, OWN), BF),
+            pltpu.VMEM((FAR, HALF, RANK), BF),
+            pltpu.VMEM((2, LAYERS, ROWS, HALF), BF),
+            pltpu.VMEM((2, LAYERS, ROWS, HALF), BF),
+            pltpu.VMEM((2, 2, LAYERS, ROWS, HALF), BF),
+            pltpu.VMEM((LAYERS, ROWS, RANK), F32),
+            pltpu.VMEM((LAYERS, ROWS, RANK), BF),
             pltpu.VMEM((NY - 1, LAYERS, ROWS // NY, RANK), BF),
             pltpu.VMEM((BLOCKS, B), F32),
             pltpu.VMEM((BLOCKS // 2, B), F32),
@@ -298,10 +357,11 @@
             pltpu.VMEM((NZ - 1, BLOCKS // 64, B), F32),
             pltpu.VMEM((BLOCKS // 64, B), F32),
             pltpu.VMEM((NY - 1, BLOCKS // 64, B), F32),
-            pltpu.SemaphoreType.DMA((2, 64)),
+            pltpu.SemaphoreType.DMA((2, 160)),
+            pltpu.SemaphoreType.DMA((NY + 1,)),
         ],
-        compiler_params=pltpu.CompilerParams(collective_id=0, has_side_effects=True, vmem_limit_bytes=32 << 20),
-    )(part)
+        compiler_params=pltpu.CompilerParams(collective_id=0, has_side_effects=True, vmem_limit_bytes=36 << 20),
+    )(omega, grads)
 
 
 def eliminate(tiles):
@@ -636,10 +696,7 @@
 
 
 def local(grad_parts, omega, first_moment, second_moment):
-    part = panel_part(omega, grad_parts[0])
-    grads, part = lax.optimization_barrier((grad_parts[0], part))
-    summed = lax.psum_scatter(grads, "dp", scatter_dimension=2, tiled=True)
-    panel, blocks = gram(part)
+    summed, panel, blocks = front(omega, grad_parts[0])
     basis = factor(blocks, panel)
     return tail(basis, summed, first_moment, second_moment)
 

time: 222 us -> 216 us (0.973)
  Pallas kernels: 190 us -> 208 us
  between operations: 14.1 us -> 0.7 us
  waiting for transfers between devices: 11.9 us -> 0 us
    pallas_call x2 -> x1, Pallas kernels: 93.3 us -> 115 us  [front(): pl.pallas_call(front_kernel, out_shape=(jax.ShapeDtypeStruct((LAYERS, ROW...]
    reduce_scatter x1 -> x0, waiting for transfers between devices: 11.9 us -> none  [local(): summed = lax.psum_scatter(grads, 'dp', scatter_dimension=2, tiled=True)]
    pallas_call x1, Pallas kernels: 67.7 us -> 64.5 us  [tail(): pl.pallas_call(tail_kernel, out_shape=(jax.ShapeDtypeStruct((8, LAYERS, O...]
  transfers between devices with their start and end apart: 1 -> 0, of which waited for: 1 -> 0; matrix products, arithmetic and copies ran while one was open for 0% -> 0% of each run, Pallas kernels for 36% -> 0%
where the time goes in v4:
time: 216 us
  Pallas kernels  208 us (96%)
  local copies, waits for them, and re-layouts  7.61 us (4%)
    pallas_call x1, Pallas kernels, front(): pl.pallas_call(front_kernel, out_shape=(jax.ShapeDtypeStruct((LAYERS, ROW...  115 us
    pallas_call x1, Pallas kernels, tail(): pl.pallas_call(tail_kernel, out_shape=(jax.ShapeDtypeStruct((8, LAYERS, O...  64.5 us
    pallas_call x1, Pallas kernels, factor(): pl.pallas_call(factor_kernel, out_shape=jax.ShapeDtypeStruct((LAYERS, ROW...  28.6 us
    unnamed x11, local copies, waits for them, and re-layouts  7.61 us

profile of v4, /device:TPU:1, one launch (start us, length us, event | category | flops | bytes accessed | tf_op | source)
XLA Modules:
  0.0 216.2 jit_solution(10936211120381892673)
XLA Ops:
  0.6 0.0 copy-start
  0.6 3.4 %copy-done = bf16[1,2,256,8192]{3,2,1,0:T(8,128)(2,1)S(1)} copy-done((bf16[1,2,256,8192]{3,2,1,0:T(8,128)(2,1)S(1)}, bf16[1,2,256,8192]{3,2,1,0:T(8,128)(2,1)}, u32[]{:S(2)}) %copy-start) | copy-done | bytes 8388632
  4.0 0.0 copy-start.1
  4.0 1.6 copy-done.1
  5.6 114.8 %shard_map.67 = (bf16[2,256,2048]{2,1,0:T(8,128)(2,1)S(1)}, bf16[2,256,512]{2,1,0:T(8,128)(2,1)S(1)}, f32[2560,128]{1,0:T(8,128)S(1)}) custom-call(bf16[2048,512]{1,0:T(8,128)(2,1)S(1)} %copy-done.1, bf16[2,256,8192]{2,1,0:T(8,128)(2,1)S(1)} %bitcast.1), custom_call_target="tpu_custom_call" | custom-call | tf_op jit(solution)/shard_map/pallas_call | solution.py:333
  120.4 0.0 copy-start.2
  120.5 0.0 copy-start.3
  120.5 28.6 %shard_map.68.basis_ref = bf16[2,256,512]{2,1,0:T(8,128)(2,1)S(1)} custom-call(f32[2560,128]{1,0:T(8,128)S(1)} %get-tuple-element.6.blocks_ref, bf16[2,256,512]{2,1,0:T(8,128)(2,1)S(1)} %get-tuple-element.7.panel_ref), custom_call_target="tpu_custom_call" | custom-call | tf_op jit(solution)/shard_map/pallas_call | solution.py:474
  149.1 0.0 copy-done.2
  149.1 0.0 copy-done.3
  149.1 64.5 %shard_map.69 = (f32[8,2,2048]{2,1,0:T(2,128)S(1)}, f32[8,2,2048]{2,1,0:T(2,128)S(1)}, bf16[2,256,2048]{2,1,0:T(8,128)(2,1)S(1)}) custom-call(bf16[2,256,512]{2,1,0:T(8,128)(2,1)S(1)} %shard_map.68.basis_ref, bf16[2,256,2048]{2,1,0:T(8,128)(2,1)S(1)} %get-tuple-element.8.summed_ref, f32[8,2,2048]{2,1,0:T(2,128)S(1)} %copy-done.2, f32[8,2,2048]{2,1,0:T(2,128)S(1)} %copy-done.3), custom_call_target="tpu_custom_call" | custom-call | tf_op jit(solution)/shard_map/pallas_call | solution.py:664
  213.6 0.7 copy.10
  214.3 0.7 copy.11
  214.9 1.3 copy.12
Async XLA Ops:
  0.6 3.4 %copy-start = (bf16[1,2,256,8192]{3,2,1,0:T(8,128)(2,1)S(1)}, bf16[1,2,256,8192]{3,2,1,0:T(8,128)(2,1)}, u32[]{:S(2)}) copy-start(bf16[1,2,256,8192]{3,2,1,0:T(8,128)(2,1)} %param.4) | copy-start | bytes 25165828
  4.0 1.6 copy-start.1
  120.4 28.7 %copy-start.2 = (f32[8,2,2048]{2,1,0:T(2,128)S(1)}, f32[8,2,2048]{2,1,0:T(2,128)}, u32[]{:S(2)}) copy-start(f32[8,2,2048]{2,1,0:T(2,128)} %first_ref.1) | copy-start | bytes 393220
  120.5 28.7 %copy-start.3 = (f32[8,2,2048]{2,1,0:T(2,128)S(1)}, f32[8,2,2048]{2,1,0:T(2,128)}, u32[]{:S(2)}) copy-start(f32[8,2,2048]{2,1,0:T(2,128)} %second_ref.1) | copy-start | bytes 393220

commit v5 on v4

v5 whole, which is shorter than its diff:
```python
import functools

import jax
import jax.numpy as jnp
from jax import lax
from jax.experimental import pallas as pl
from jax.experimental.pallas import tpu as pltpu
from jax.sharding import PartitionSpec as P

HIGHEST = lax.Precision.HIGHEST
MESH = pl.DeviceIdType.MESH
NT = (((1,), (1,)), ((), ()))
TN = (((0,), (0,)), ((), ()))
BF = jnp.bfloat16
F32 = jnp.float32

LAYERS = 2
ROWS = 256
D = 8192
OWN = 2048
HALF = 1024
RANK = 512
B = 128
NY, NX, NZ, NC = 4, 4, 8, 2


def place():
    mp = lax.axis_index("mp")
    return lax.axis_index("dp"), mp // (NZ * NC), (mp // NC) % NZ, mp % NC


def device(y, x, z, c):
    return {"dp": y, "mp": x * (NZ * NC) + z * NC + c}


def greet(peers):
    barrier = pltpu.get_barrier_semaphore()
    for peer in peers:
        pl.semaphore_signal(barrier, inc=1, device_id=peer, device_id_type=MESH)
    pl.semaphore_wait(barrier, len(peers))


def along(axis, spot, k):
    y, x, z, c = spot
    if axis == "y":
        return device((y + k) % NY, x, z, c)
    if axis == "x":
        return device(y, (x + k) % NX, z, c)
    if axis == "z":
        return device(y, x, (z + k) % NZ, c)
    return device(y, x, z, 1 - c)


def ship(src, dst, send, recv, peer):
    copy = pltpu.make_async_remote_copy(
        src_ref=src, dst_ref=dst, send_sem=send, recv_sem=recv, device_id=peer, device_id_type=MESH
    )
    copy.start()
    return copy


def span(start, size):
    return pl.ds(pl.multiple_of(start, size), size)


def eliminate(whole):
    lane = lax.broadcasted_iota(jnp.int32, (1, 8, B), 2)
    sub = lax.broadcasted_iota(jnp.int32, (1, 8, B), 1)
    sub4 = lax.broadcasted_iota(jnp.int32, (1, 1, 8, B), 2)
    found = []
    for b in range(B // 8):
        inside = (lane >= 8 * b) & (lane < 8 * b + 8)
        top = whole[:, :8, :]
        cols = [top[:, :, 8 * b + k : 8 * b + k + 1] for k in range(8)]
        cols = jnp.stack([jnp.broadcast_to(col, (LAYERS, 8, B)) for col in cols], axis=1)
        start = jnp.where(inside, (lane == sub + 8 * b).astype(F32), top)
        state = jnp.concatenate([cols, start[:, None]], axis=1)
        forward = start
        scale = jnp.zeros((LAYERS, 8, B), F32)
        for k in range(8):
            column = state[:, k]
            pivot = column[:, k : k + 1, :]
            inverse = 1.0 / pivot
            factor = column * inverse
            line = state[:, :, k : k + 1, :]
            state = jnp.where(sub4 == k, line * inverse[:, None], state - factor[:, None] * line)
            forward = jnp.where(sub > k, forward - factor * forward[:, k : k + 1, :], forward)
            scale = jnp.where(sub == k, pivot, scale)
        found.append(jnp.where(lane < 8 * b + 8, forward, 0.0) * lax.rsqrt(scale))
        if b < B // 8 - 1:
            rest = whole[:, 8:, :]
            total = None
            for k in range(8):
                term = rest[:, :, 8 * b + k : 8 * b + k + 1] * state[:, 8, k : k + 1, :]
                total = term if total is None else total + term
            whole = jnp.where(inside[:, :1], 0.0, rest) - total
    return jnp.concatenate(found, axis=1)


STREAMS = ((0, 1024), (1024, 1536))
BLOCKS = LAYERS * 10 * B
FAR = NY - 1


def rows_at(start, size):
    return pl.ds(pl.multiple_of(start, 8), size)


def front_kernel(
    omega_hbm,
    grads_hbm,
    summed_ref,
    basis_ref,
    panel_ref,
    blocks_ref,
    w,
    inv,
    omega_ref,
    grads,
    omegas,
    relay_in,
    joint,
    near_in,
    partial,
    part,
    rs_buf,
    mine,
    core_buf,
    chip,
    x_buf,
    x_sum,
    z_buf,
    strip,
    y_buf,
    sems,
    local_sems,
):
    spot = place()
    y, x, z, c = spot
    twin = along("c", spot, 1)
    near_y = [along("y", spot, k) for k in range(1, NY)]
    near_x = [along("x", spot, k) for k in range(1, NX)]
    near_z = [along("z", spot, k) for k in range(1, NZ)]
    loads = [pltpu.make_async_copy(omega_hbm, omega_ref, local_sems.at[NY])]
    loads[0].start()
    for k in (0, 1, 3, 2):
        columns = span(((y + k) % NY) * OWN, OWN)
        load = pltpu.make_async_copy(grads_hbm.at[:, :, columns], grads.at[k], local_sems.at[k])
        load.start()
        loads.append(load)
    greet([twin] + near_y + near_x + near_z)
    done, sent = [], []
    count = [0]

    def go(src, dst, peer):
        copy = ship(src, dst, sems.at[0, count[0]], sems.at[1, count[0]], peer)
        count[0] += 1
        done.append(copy)
        return copy

    def landed(copies):
        for copy in copies:
            copy.wait_recv()

    relays, nears = [None] * 2, [None] * 2

    SUB = ROWS // 2

    def columns(part_of, k):
        return span(((y + k) % NY) * OWN + (1 - part_of) * HALF, HALF)

    def launch(part_of):
        relays[part_of] = [
            [
                go(
                    grads_hbm.at[n, pl.ds(r * SUB, SUB), columns(part_of, 2)],
                    relay_in.at[part_of, n, pl.ds(r * SUB, SUB), :],
                    near_y[2 * n],
                )
                for n in range(2)
            ]
            for r in range(2)
        ]

    def launch_near(part_of):
        for copies in relays[part_of]:
            for copy in copies:
                copy.wait_send()
                sent.append(id(copy))
        nears[part_of] = [
            go(grads_hbm.at[1, :, columns(part_of, 1)], near_in.at[part_of, 0, 1], near_y[0]),
            go(grads_hbm.at[0, :, columns(part_of, 3)], near_in.at[part_of, 1, 0], near_y[2]),
        ]

    def in_rows(first_row, count_rows, work):
        def body(t, carry):
            work(pl.ds(pl.multiple_of(first_row + t * 32, 32), 32))
            return carry

        lax.fori_loop(0, count_rows // 32, body, 0)

    def combine(part_of):
        off = (1 - part_of) * HALF
        for r in range(2):
            for n, k in ((0, 1), (1, 3)):
                relays[part_of][r][n].wait_recv()

                def work(at):
                    own_term = grads[k, n, at, off : off + HALF].astype(F32)
                    joint[part_of, n, at, :] = (own_term + relay_in[part_of, n, at, :].astype(F32)).astype(BF)

                in_rows(r * SUB, SUB, work)
                at = pl.ds(r * SUB, SUB)
                nears[part_of].append(go(joint.at[part_of, n, at, :], near_in.at[part_of, n, n, at, :], near_y[k - 1]))

    def finish_sum(part_of):
        off = (1 - part_of) * HALF
        landed(nears[part_of])

        def work(at):
            for n in range(LAYERS):
                out = grads[0, n, at, off : off + HALF].astype(F32) + near_in[part_of, 0, n, at, :].astype(F32)
                summed_ref[n, at, off : off + HALF] = (out + near_in[part_of, 1, n, at, :].astype(F32)).astype(BF)

        in_rows(0, ROWS, work)

    strip_at = span(x * 256 + c * B + z * 16, 16)
    slices = [go(omega_hbm.at[strip_at, :], omegas.at[FAR - k, strip_at, :], near_y[k - 1]) for k in range(1, NY)]
    launch(0)

    def block(s, which, start, size):
        return omegas.at[s, pl.ds(pl.multiple_of(which * 256 + c * B + start, size), size), :]

    flights = []
    for s in range(FAR):
        slices[FAR - 1 - s].wait_recv()
        piece = omegas.at[s, strip_at, :]
        flights.append([go(piece, piece, peer) for peer in near_z])
    for load in loads:
        load.wait()
    for n in range(LAYERS):
        partial[n] = jnp.dot(grads[0, n, :, :HALF], omega_ref[:HALF, :], preferred_element_type=F32)
    launch_near(0)
    up, down = near_x[0], near_x[2]
    above, below, across = (x + 1) % NX, (x + NX - 1) % NX, (x + 2) % NX
    h = B // 2
    firsts, crossed, seconds = [], [], []
    for s in range(FAR):
        landed(flights[s])
        low, high, whole = block(s, x, 0, h), block(s, x, h, h), block(s, x, 0, B)
        firsts.append([go(low, low, up), go(high, high, down), go(high, high, up), go(low, low, down)])
        crossed.append([go(whole, whole, twin)])
    combine(0)
    for s in range(FAR):
        firsts[s][0].wait_recv()
        low = block(s, below, 0, h)
        seconds.append([go(low, low, up)])
        firsts[s][1].wait_recv()
        high = block(s, above, h, h)
        seconds[s].append(go(high, high, down))
        landed(firsts[s][2:])
        for which in (below, above):
            whole = block(s, which, 0, B)
            crossed[s].append(go(whole, whole, twin))
    for s in range(FAR):
        landed(seconds[s])
        whole = block(s, across, 0, B)
        crossed[s].append(go(whole, whole, twin))
    for s in range(FAR):
        landed(crossed[s])
        for n in range(LAYERS):
            partial[n] += jnp.dot(grads[s + 1, n, :, :HALF], omegas[s], preferred_element_type=F32)
    finish_sum(0)
    for n in range(LAYERS):
        out = partial[n] + jnp.dot(summed_ref[n, :, HALF:], omega_ref[HALF:, :], preferred_element_type=F32)
        part[n] = out.astype(BF)

    q = ROWS // NY
    own = span(y * q, q)
    first = [
        [
            go(part.at[n, span(((y + k) % NY) * q, q), :], rs_buf.at[k - 1, n], near_y[k - 1])
            for k in range(1, NY)
        ]
        for n in range(LAYERS)
    ]
    spread = []
    for n in range(LAYERS):
        landed(first[n])
        if n == 1:
            launch(1)
        total = part[n, own, :].astype(F32)
        for k in range(1, NY):
            total = total + rs_buf[k - 1, n].astype(F32)
        panel_ref[n, own, :] = total.astype(BF)
        whole = panel_ref[n, own, :]
        row = n * 10 * B
        for i in range(4):
            wide = (i + 1) * B
            out = lax.dot_general(whole[:, i * B : wide], whole[:, :wide], TN, preferred_element_type=F32)
            for j in range(i + 1):
                mine[row : row + B, :] = out[:, j * B : j * B + B]
                row += B
        if n == 0:
            start, size = STREAMS[0]
            half = size // 2
            flight = [
                [go(mine.at[rows_at(start + (1 - c) * half, half), :], core_buf.at[pl.ds(start // 2, half), :], twin)]
            ]
    start, size = STREAMS[1]
    half = size // 2
    flight.append(
        [go(mine.at[rows_at(start + (1 - c) * half, half), :], core_buf.at[pl.ds(start // 2, half), :], twin)]
    )

    for s, (start, size) in enumerate(STREAMS):
        half, quarter = size // 2, size // 8
        landed(flight[s])
        here = pl.ds(start // 2, half)
        chip[here, :] = mine[rows_at(start + c * half, half), :] + core_buf[here, :]
        flight[s] = [
            go(
                chip.at[rows_at(start // 2 + ((x + k) % NX) * quarter, quarter), :],
                x_buf.at[k - 1, pl.ds(start // 8, quarter), :],
                near_x[k - 1],
            )
            for k in range(1, NX)
        ]
    for s, (start, size) in enumerate(STREAMS):
        quarter, piece = size // 8, size // 64
        landed(flight[s])
        total = chip[rows_at(start // 2 + x * quarter, quarter), :]
        for k in range(1, NX):
            total = total + x_buf[k - 1, start // 8 : start // 8 + quarter, :]
        x_sum[start // 8 : start // 8 + quarter, :] = total
        flight[s] = [
            go(
                x_sum.at[rows_at(start // 8 + ((z + k) % NZ) * piece, piece), :],
                z_buf.at[k - 1, pl.ds(start // 64, piece), :],
                near_z[k - 1],
            )
            for k in range(1, NZ)
        ]
    for s, (start, size) in enumerate(STREAMS):
        piece = size // 64
        landed(flight[s])
        here = pl.ds(start // 64, piece)
        total = x_sum[rows_at(start // 8 + z * piece, piece), :]
        for k in range(1, NZ):
            total = total + z_buf[k - 1, here, :]
        strip[here, :] = total
        flight[s] = [go(strip.at[here, :], y_buf.at[k - 1, here, :], near_y[k - 1]) for k in range(1, NY)]
    for s, (start, size) in enumerate(STREAMS):
        half, quarter, piece = size // 2, size // 8, size // 64
        landed(flight[s])
        here = pl.ds(start // 64, piece)
        total = strip[here, :]
        for k in range(1, NY):
            total = total + y_buf[k - 1, here, :]
        at = rows_at(start + c * half + x * quarter + z * piece, piece)
        blocks_ref[at, :] = total
        flight[s] = [go(blocks_ref.at[at, :], blocks_ref.at[at, :], peer) for peer in near_z]
    for k in range(1, NY):
        spread.append(go(panel_ref.at[:, own, :], panel_ref.at[:, own, :], near_y[k - 1]))
    launch_near(1)
    combine(1)
    for s, (start, size) in enumerate(STREAMS):
        half, quarter = size // 2, size // 8
        landed(flight[s])
        at = rows_at(start + c * half + x * quarter, quarter)
        flight[s] = [go(blocks_ref.at[at, :], blocks_ref.at[at, :], peer) for peer in near_x]
    for s, (start, size) in enumerate(STREAMS):
        half = size // 2
        landed(flight[s])
        at = rows_at(start + c * half, half)
        flight[s] = [go(blocks_ref.at[at, :], blocks_ref.at[at, :], twin)]
    for copies in flight:
        landed(copies)
    for n in range(LAYERS):
        row = n * 10 * B
        for i in range(4):
            for j in range(i + 1):
                block = blocks_ref[row : row + B, :]
                row += B
                w[n, i * B : i * B + B, j * B : j * B + B] = block
                if i != j:
                    w[n, j * B : j * B + B, i * B : i * B + B] = block.T

    def step(k, carry):
        here = span(k * B, B)
        inv[...] = eliminate(w[:, here, here])
        for at in range(4):

            @pl.when(k == at)
            def _():
                a, z = at * B, at * B + B
                for n in range(LAYERS):
                    inverse = inv[n]
                    right = jnp.dot(inverse, w[n, a:z, :], precision=HIGHEST, preferred_element_type=F32)
                    pieces = [right[:, :a], inverse, right[:, z:]]
                    right = jnp.concatenate([p for p in pieces if p.shape[1]], axis=1)
                    if z < RANK:
                        left = lax.dot_general(
                            w[n, z:, a:z], inverse, NT, precision=HIGHEST, preferred_element_type=F32
                        )
                        w[n, z:, a:z] = jnp.zeros((RANK - z, B), F32)
                        w[n, z:, :] = w[n, z:, :] - jnp.dot(
                            left, right, precision=HIGHEST, preferred_element_type=F32
                        )
                        right = jnp.concatenate([right[:, :z], jnp.zeros((B, RANK - z), F32)], axis=1)
                    w[n, a:z, :] = right

        return carry

    lax.fori_loop(0, 4, step, 0)
    landed(spread)
    for n in range(LAYERS):
        rest = w[n]
        basis = jnp.zeros((ROWS, RANK), F32)
        for _ in range(3):
            part = rest.astype(BF)
            rest = rest - part.astype(F32)
            basis = basis + lax.dot_general(panel_ref[n], part, NT, preferred_element_type=F32)
        basis_ref[n] = basis.astype(BF)
    finish_sum(1)
    for copy in done:
        if id(copy) not in sent:
            copy.wait_send()


def front(omega, grads):
    vmem = pl.BlockSpec(memory_space=pltpu.VMEM)
    return pl.pallas_call(
        front_kernel,
        out_shape=(
            jax.ShapeDtypeStruct((LAYERS, ROWS, OWN), BF),
            jax.ShapeDtypeStruct((LAYERS, ROWS, RANK), BF),
        ),
        in_specs=[pl.BlockSpec(memory_space=pltpu.HBM)] * 2,
        out_specs=(vmem, vmem),
        scratch_shapes=[
            pltpu.VMEM((LAYERS, ROWS, RANK), BF),
            pltpu.VMEM((BLOCKS, B), F32),
            pltpu.VMEM((LAYERS, RANK, RANK), F32),
            pltpu.VMEM((LAYERS, B, B), F32),
            pltpu.VMEM((OWN, RANK), BF),
            pltpu.VMEM((NY, LAYERS, ROWS, OWN), BF),
            pltpu.VMEM((FAR, HALF, RANK), BF),
            pltpu.VMEM((2, LAYERS, ROWS, HALF), BF),
            pltpu.VMEM((2, LAYERS, ROWS, HALF), BF),
            pltpu.VMEM((2, 2, LAYERS, ROWS, HALF), BF),
            pltpu.VMEM((LAYERS, ROWS, RANK), F32),
            pltpu.VMEM((LAYERS, ROWS, RANK), BF),
            pltpu.VMEM((NY - 1, LAYERS, ROWS // NY, RANK), BF),
            pltpu.VMEM((BLOCKS, B), F32),
            pltpu.VMEM((BLOCKS // 2, B), F32),
            pltpu.VMEM((BLOCKS // 2, B), F32),
            pltpu.VMEM((NX - 1, BLOCKS // 8, B), F32),
            pltpu.VMEM((BLOCKS // 8, B), F32),
            pltpu.VMEM((NZ - 1, BLOCKS // 64, B), F32),
            pltpu.VMEM((BLOCKS // 64, B), F32),
            pltpu.VMEM((NY - 1, BLOCKS // 64, B), F32),
            pltpu.SemaphoreType.DMA((2, 160)),
            pltpu.SemaphoreType.DMA((NY + 1,)),
        ],
        compiler_params=pltpu.CompilerParams(collective_id=0, has_side_effects=True, vmem_limit_bytes=50 << 20),
    )(omega, grads)


RUNS = ((0, 0), (1, 0), (0, 512), (1, 512))
WIDE = 512


def tail_kernel(
    basis_ref,
    summed_ref,
    first_ref,
    second_ref,
    new_first_ref,
    new_second_ref,
    delta_ref,
    summed,
    twin_basis,
    twin_summed,
    twin_first,
    twin_second,
    back_first,
    back_second,
    relay_out,
    relay_in,
    near_out,
    near_in,
    x_own,
    z_out,
    z_in,
    z_own,
    joined,
    gathered,
    sems,
    local_sems,
):
    spot = place()
    y, x, z, c = spot
    twin = along("c", spot, 1)
    up, down = along("x", spot, 1), along("x", spot, NX - 1)
    near_z = [along("z", spot, k) for k in range(1, NZ)]
    mine, other = span(c * HALF, HALF), span((1 - c) * HALF, HALF)
    runs = range(len(RUNS))

    def cut(core, r):
        return pl.ds(pl.multiple_of(core * HALF + RUNS[r][1], WIDE), WIDE)

    loads = []
    for r in runs:
        load = pltpu.make_async_copy(summed_ref.at[RUNS[r][0], :, cut(c, r)], summed.at[r], local_sems.at[r])
        load.start()
        loads.append(load)
    greet([twin, up, down] + near_z)
    done = []
    count = [0]

    def go(src, dst, peer):
        copy = ship(src, dst, sems.at[0, count[0]], sems.at[1, count[0]], peer)
        count[0] += 1
        done.append(copy)
        return copy

    def landed(copies):
        for copy in copies:
            copy.wait_recv()

    got = []
    for r in runs:
        copies = [go(summed_ref.at[RUNS[r][0], :, cut(1 - c, r)], twin_summed.at[r], twin)]
        if r < LAYERS:
            copies.append(go(basis_ref.at[r], twin_basis.at[r], twin))
        got.append(copies)
    moments = [
        go(first_ref.at[:, :, other], twin_first, twin),
        go(second_ref.at[:, :, other], twin_second, twin),
    ]

    def product(r, start, size):
        here, n = span(start, size), RUNS[r][0]
        out = lax.dot_general(basis_ref[n, :, here], summed[r], TN, preferred_element_type=F32)
        return out + lax.dot_general(twin_basis[n, :, here], twin_summed[r], TN, preferred_element_type=F32)

    h = B // 2
    above, below, across = ((x + 1) % NX) * B, ((x + NX - 1) % NX) * B, ((x + 2) % NX) * B
    relays, nears, spreads, firsts, seconds = {}, {}, {}, {}, {}
    z_copies, crossed = {}, {}
    slot = span(x * B + z * 16, 16)
    ours, theirs = span(c * 8, 8), span((1 - c) * 8, 8)

    def part(n, start, size):
        return gathered.at[c, n, pl.ds(pl.multiple_of(start, size), size), :]

    def multiply(n):
        landed(got[n])
        loads[n].wait()
        far = product(n, across, B)
        relay_out[n, 0] = far[:h].astype(BF)
        relay_out[n, 1] = far[h:].astype(BF)
        relays[n] = [go(relay_out.at[n, 0], relay_in.at[n, 0], up), go(relay_out.at[n, 1], relay_in.at[n, 1], down)]
        x_own[n, 1] = product(n, above, B)
        near_out[n, 0, h:, :] = x_own[n, 1, h:, :].astype(BF)
        nears[n] = [go(near_out.at[n, 0, pl.ds(h, h), :], near_in.at[n, 0, pl.ds(h, h), :], up)]
        x_own[n, 2] = product(n, below, B)
        near_out[n, 1, :h, :] = x_own[n, 2, :h, :].astype(BF)
        nears[n].append(go(near_out.at[n, 1, pl.ds(0, h), :], near_in.at[n, 1, pl.ds(0, h), :], down))
        x_own[n, 0] = product(n, x * B, B)

    def pass_on(n):
        relays[n][0].wait_recv()
        near_out[n, 0, :h, :] = (x_own[n, 1, :h, :] + relay_in[n, 0].astype(F32)).astype(BF)
        nears[n].append(go(near_out.at[n, 0, pl.ds(0, h), :], near_in.at[n, 0, pl.ds(0, h), :], up))
        relays[n][1].wait_recv()
        near_out[n, 1, h:, :] = (x_own[n, 2, h:, :] + relay_in[n, 1].astype(F32)).astype(BF)
        nears[n].append(go(near_out.at[n, 1, pl.ds(h, h), :], near_in.at[n, 1, pl.ds(h, h), :], down))

    def over_z(n):
        landed(nears[n])
        total = x_own[n, 0] + near_in[n, 0].astype(F32) + near_in[n, 1].astype(F32)
        x_own[n, 0] = total
        z_out[n] = total.astype(BF)
        z_copies[n] = [
            go(z_out.at[n, span(((z + k) % NZ) * 16, 16), :], z_in.at[n, k - 1], near_z[k - 1]) for k in range(1, NZ)
        ]

    def adam(projected, first, second):
        new_first = 0.9 * first + 0.1 * projected
        new_second = 0.999 * second + 0.001 * projected * projected
        return new_first, new_second, new_first / (jnp.sqrt(new_second) + 1e-08)

    def update(n):
        layer, off = RUNS[n]
        here, there = cut(c, n), pl.ds(off, WIDE)
        if n == 0:
            landed(moments)
        landed(z_copies[n])
        total = x_own[n, 0, span(z * 16, 16), :]
        for k in range(1, NZ):
            total = total + z_in[n, k - 1].astype(F32)
        z_own[n] = total
        new_first, new_second, fresh = adam(z_own[n, ours, :], first_ref[:, layer, here], second_ref[:, layer, here])
        new_first_ref[:, layer, here] = new_first
        new_second_ref[:, layer, here] = new_second
        joined[n, ours, :] = fresh
        new_first, new_second, fresh = adam(z_own[n, theirs, :], twin_first[:, layer, there], twin_second[:, layer, there])
        back_first[:, layer, there] = new_first
        back_second[:, layer, there] = new_second
        joined[n, theirs, :] = fresh
        gathered[c, n, slot, :] = joined[n].astype(BF)
        piece = gathered.at[c, n, slot, :]
        spreads[n] = [go(piece, piece, peer) for peer in near_z]

    def over_x(n):
        landed(spreads[n])
        low, high, whole = part(n, x * B, h), part(n, x * B + h, h), part(n, x * B, B)
        firsts[n] = [go(low, low, up), go(high, high, down), go(high, high, up), go(low, low, down)]
        crossed[n] = [go(whole, whole, twin)]

    def forward(n):
        firsts[n][0].wait_recv()
        low = part(n, below, h)
        seconds[n] = [go(low, low, up)]
        firsts[n][1].wait_recv()
        high = part(n, above + h, h)
        seconds[n].append(go(high, high, down))
        landed(firsts[n][2:])
        for start in (below, above):
            whole = part(n, start, B)
            crossed[n].append(go(whole, whole, twin))

    def cross(n):
        landed(seconds[n])
        whole = part(n, across, B)
        crossed[n].append(go(whole, whole, twin))

    def apply(n):
        layer, off = RUNS[n]
        landed(crossed[n])
        for core in range(NC):
            out = jnp.dot(basis_ref[layer], gathered[core, n], preferred_element_type=F32)
            delta_ref[layer, :, core * HALF + off : core * HALF + off + WIDE] = out.astype(BF)

    stages = (multiply, pass_on, over_z, update, over_x, forward, cross, apply)
    for tick in range(len(RUNS) + len(stages) - 1):
        for lag, stage in enumerate(stages):
            if 0 <= tick - lag < len(RUNS):
                stage(tick - lag)
    backs = [
        go(back_first, new_first_ref.at[:, :, mine], twin),
        go(back_second, new_second_ref.at[:, :, mine], twin),
    ]
    landed(backs)
    for copy in done:
        copy.wait_send()


def tail(basis, summed, first, second):
    vmem = pl.BlockSpec(memory_space=pltpu.VMEM)
    return pl.pallas_call(
        tail_kernel,
        out_shape=(
            jax.ShapeDtypeStruct((8, LAYERS, OWN), F32),
            jax.ShapeDtypeStruct((8, LAYERS, OWN), F32),
            jax.ShapeDtypeStruct((LAYERS, ROWS, OWN), BF),
        ),
        in_specs=[vmem, pl.BlockSpec(memory_space=pl.ANY), vmem, vmem],
        out_specs=(vmem,) * 3,
        scratch_shapes=[
            pltpu.VMEM((4, ROWS, WIDE), BF),
            pltpu.VMEM((LAYERS, ROWS, RANK), BF),
            pltpu.VMEM((4, ROWS, WIDE), BF),
            pltpu.VMEM((8, LAYERS, HALF), F32),
            pltpu.VMEM((8, LAYERS, HALF), F32),
            pltpu.VMEM((8, LAYERS, HALF), F32),
            pltpu.VMEM((8, LAYERS, HALF), F32),
            pltpu.VMEM((4, 2, B // 2, WIDE), BF),
            pltpu.VMEM((4, 2, B // 2, WIDE), BF),
            pltpu.VMEM((4, 2, B, WIDE), BF),
            pltpu.VMEM((4, 2, B, WIDE), BF),
            pltpu.VMEM((4, 3, B, WIDE), F32),
            pltpu.VMEM((4, B, WIDE), BF),
            pltpu.VMEM((4, NZ - 1, 16, WIDE), BF),
            pltpu.VMEM((4, 16, WIDE), F32),
            pltpu.VMEM((4, 16, WIDE), F32),
            pltpu.VMEM((NC, 4, RANK, WIDE), BF),
            pltpu.SemaphoreType.DMA((2, 144)),
            pltpu.SemaphoreType.DMA((4,)),
        ],
        compiler_params=pltpu.CompilerParams(collective_id=1, has_side_effects=True, vmem_limit_bytes=48 << 20),
    )(basis, summed, first, second)


def local(grad_parts, omega, first_moment, second_moment):
    summed, basis = front(omega, grad_parts[0])
    return tail(basis, summed, first_moment, second_moment)


def solution(mesh):
    return jax.shard_map(
        local,
        mesh=mesh,
        in_specs=(P("dp", None, "mp", None), P("dp", None), P("mp", None, "dp"), P("mp", None, "dp")),
        out_specs=(P("mp", None, "dp"), P("mp", None, "dp"), P(None, "mp", "dp")),
        check_vma=False,
    )
```

time: 216 us -> 174 us (0.81)
  Pallas kernels: 208 us -> 171 us
  local copies, waits for them, and re-layouts: 7.61 us -> 2.64 us
    pallas_call x1 -> x0, Pallas kernels: 28.6 us -> none  [factor(): pl.pallas_call(factor_kernel, out_shape=jax.ShapeDtypeStruct((LAYERS, ROW...]
    pallas_call x1, Pallas kernels: 64.5 us -> 55.5 us  [tail(): pl.pallas_call(tail_kernel, out_shape=(jax.ShapeDtypeStruct((8, LAYERS, O...]
    unnamed x11 -> x7, local copies, waits for them, and re-layouts: 7.61 us -> 2.64 us
where the time goes in v5:
time: 174 us
  Pallas kernels  171 us (98%)
  local copies, waits for them, and re-layouts  2.64 us (2%)
    pallas_call x1, Pallas kernels, front(): pl.pallas_call(front_kernel, out_shape=(jax.ShapeDtypeStruct((LAYERS, ROW...  115 us
    pallas_call x1, Pallas kernels, tail(): pl.pallas_call(tail_kernel, out_shape=(jax.ShapeDtypeStruct((8, LAYERS, O...  55.5 us

profile of v5, /device:TPU:1, one launch (start us, length us, event | category | flops | bytes accessed | tf_op | source)
XLA Modules:
  0.0 174.2 jit_solution(16921845156184365554)
XLA Ops:
  0.6 0.0 copy-start
  0.6 0.0 copy-start.1
  0.7 115.3 %shard_map.67 = (bf16[2,256,2048]{2,1,0:T(8,128)(2,1)S(1)}, bf16[2,256,512]{2,1,0:T(8,128)(2,1)S(1)}) custom-call(bf16[2048,512]{1,0:T(8,128)(2,1)} %omega_hbm.1, bf16[2,256,8192]{2,1,0:T(8,128)(2,1)} %bitcast.1), custom_call_target="tpu_custom_call" | custom-call | tf_op jit(solution)/shard_map/pallas_call | solution.py:433
  116.0 0.0 copy-done
  116.0 0.0 copy-done.1
  116.0 55.5 %shard_map.68 = (f32[8,2,2048]{2,1,0:T(2,128)S(1)}, f32[8,2,2048]{2,1,0:T(2,128)S(1)}, bf16[2,256,2048]{2,1,0:T(8,128)(2,1)S(1)}) custom-call(bf16[2,256,512]{2,1,0:T(8,128)(2,1)S(1)} %get-tuple-element.5.basis_ref, bf16[2,256,2048]{2,1,0:T(8,128)(2,1)S(1)} %get-tuple-element.6.summed_ref, f32[8,2,2048]{2,1,0:T(2,128)S(1)} %copy-done, ...), custom_call_target="tpu_custom_call" | custom-call | tf_op jit(solution)/shard_map/pallas_call | solution.py:663
  171.5 0.7 copy.10
  172.2 0.7 copy.11
  172.8 1.3 copy.12
Async XLA Ops:
  0.6 115.3 %copy-start = (f32[8,2,2048]{2,1,0:T(2,128)S(1)}, f32[8,2,2048]{2,1,0:T(2,128)}, u32[]{:S(2)}) copy-start(f32[8,2,2048]{2,1,0:T(2,128)} %first_ref.1) | copy-start | bytes 393220
  0.6 115.3 %copy-start.1 = (f32[8,2,2048]{2,1,0:T(2,128)S(1)}, f32[8,2,2048]{2,1,0:T(2,128)}, u32[]{:S(2)}) copy-start(f32[8,2,2048]{2,1,0:T(2,128)} %second_ref.1) | copy-start | bytes 393220

commit v6 on v5

--- a/solution.py
+++ b/solution.py
@@ -61,6 +61,160 @@
 
 def span(start, size):
     return pl.ds(pl.multiple_of(start, size), size)
+
+
+RUNS = ((0, 0), (1, 0), (0, 512), (1, 512))
+WIDE = 512
+
+
+def cut(core, r):
+    return pl.ds(pl.multiple_of(core * HALF + RUNS[r][1], WIDE), WIDE)
+
+
+def finish(spot, go, landed, moments, got, refs, held, scratch):
+    y, x, z, c = spot
+    first_ref, second_ref, new_first_ref, new_second_ref, delta_ref = refs
+    summed_ref, basis_ref, x_own = held
+    (
+        twin_basis,
+        twin_summed,
+        twin_first,
+        twin_second,
+        back_first,
+        back_second,
+        relay_out,
+        relay_in,
+        near_out,
+        near_in,
+        z_out,
+        z_in,
+        z_own,
+        joined,
+        gathered,
+    ) = scratch
+    twin = along("c", spot, 1)
+    up, down = along("x", spot, 1), along("x", spot, NX - 1)
+    near_z = [along("z", spot, k) for k in range(1, NZ)]
+    mine = span(c * HALF, HALF)
+
+    def product(r, start, size):
+        here, n = span(start, size), RUNS[r][0]
+        out = lax.dot_general(basis_ref[n, :, here], summed_ref[n, :, cut(c, r)], TN, preferred_element_type=F32)
+        return out + lax.dot_general(twin_basis[n, :, here], twin_summed[r], TN, preferred_element_type=F32)
+
+    h = B // 2
+    above, below, across = ((x + 1) % NX) * B, ((x + NX - 1) % NX) * B, ((x + 2) % NX) * B
+    relays, nears, spreads, firsts, seconds = {}, {}, {}, {}, {}
+    z_copies, crossed = {}, {}
+    slot = span(x * B + z * 16, 16)
+    ours, theirs = span(c * 8, 8), span((1 - c) * 8, 8)
+
+    def part(n, start, size):
+        return gathered.at[c, n, pl.ds(pl.multiple_of(start, size), size), :]
+
+    def kept(n, start, size):
+        return slice((n % 2) * 2 * B + start, (n % 2) * 2 * B + start + size)
+
+    def multiply(n):
+        landed(got[n])
+        far = product(n, across, B)
+        relay_out[n, 0] = far[:h].astype(BF)
+        relay_out[n, 1] = far[h:].astype(BF)
+        relays[n] = [go(relay_out.at[n, 0], relay_in.at[n, 0], up), go(relay_out.at[n, 1], relay_in.at[n, 1], down)]
+        out = product(n, above, B)
+        x_own[n // 2, kept(n, B, h), :] = out[:h]
+        near_out[n, 0, h:, :] = out[h:].astype(BF)
+        nears[n] = [go(near_out.at[n, 0, pl.ds(h, h), :], near_in.at[n, 0, pl.ds(h, h), :], up)]
+        out = product(n, below, B)
+        x_own[n // 2, kept(n, B + h, h), :] = out[h:]
+        near_out[n, 1, :h, :] = out[:h].astype(BF)
+        nears[n].append(go(near_out.at[n, 1, pl.ds(0, h), :], near_in.at[n, 1, pl.ds(0, h), :], down))
+        x_own[n // 2, kept(n, 0, B), :] = product(n, x * B, B)
+
+    def pass_on(n):
+        relays[n][0].wait_recv()
+        near_out[n, 0, :h, :] = (x_own[n // 2, kept(n, B, h), :] + relay_in[n, 0].astype(F32)).astype(BF)
+        nears[n].append(go(near_out.at[n, 0, pl.ds(0, h), :], near_in.at[n, 0, pl.ds(0, h), :], up))
+        relays[n][1].wait_recv()
+        near_out[n, 1, h:, :] = (x_own[n // 2, kept(n, B + h, h), :] + relay_in[n, 1].astype(F32)).astype(BF)
+        nears[n].append(go(near_out.at[n, 1, pl.ds(h, h), :], near_in.at[n, 1, pl.ds(h, h), :], down))
+
+    def over_z(n):
+        landed(nears[n])
+        total = x_own[n // 2, kept(n, 0, B), :] + near_in[n, 0].astype(F32) + near_in[n, 1].astype(F32)
+        x_own[n // 2, kept(n, 0, B), :] = total
+        z_out[n] = total.astype(BF)
+        z_copies[n] = [
+            go(z_out.at[n, span(((z + k) % NZ) * 16, 16), :], z_in.at[n, k - 1], near_z[k - 1]) for k in range(1, NZ)
+        ]
+
+    def adam(projected, first, second):
+        new_first = 0.9 * first + 0.1 * projected
+        new_second = 0.999 * second + 0.001 * projected * projected
+        return new_first, new_second, new_first / (jnp.sqrt(new_second) + 1e-08)
+
+    def update(n):
+        layer, off = RUNS[n]
+        here, there = cut(c, n), pl.ds(off, WIDE)
+        if n == 0:
+            landed(moments)
+        landed(z_copies[n])
+        total = x_own[n // 2, pl.ds(pl.multiple_of((n % 2) * 2 * B + z * 16, 16), 16), :]
+        for k in range(1, NZ):
+            total = total + z_in[n, k - 1].astype(F32)
+        z_own[n] = total
+        new_first, new_second, fresh = adam(z_own[n, ours, :], first_ref[:, layer, here], second_ref[:, layer, here])
+        new_first_ref[:, layer, here] = new_first
+        new_second_ref[:, layer, here] = new_second
+        joined[n, ours, :] = fresh
+        new_first, new_second, fresh = adam(z_own[n, theirs, :], twin_first[:, layer, there], twin_second[:, layer, there])
+        back_first[:, layer, there] = new_first
+        back_second[:, layer, there] = new_second
+        joined[n, theirs, :] = fresh
+        gathered[c, n, slot, :] = joined[n].astype(BF)
+        piece = gathered.at[c, n, slot, :]
+        spreads[n] = [go(piece, piece, peer) for peer in near_z]
+
+    def over_x(n):
+        landed(spreads[n])
+        low, high, whole = part(n, x * B, h), part(n, x * B + h, h), part(n, x * B, B)
+        firsts[n] = [go(low, low, up), go(high, high, down), go(high, high, up), go(low, low, down)]
+        crossed[n] = [go(whole, whole, twin)]
+
+    def forward(n):
+        firsts[n][0].wait_recv()
+        low = part(n, below, h)
+        seconds[n] = [go(low, low, up)]
+        firsts[n][1].wait_recv()
+        high = part(n, above + h, h)
+        seconds[n].append(go(high, high, down))
+        landed(firsts[n][2:])
+        for start in (below, above):
+            whole = part(n, start, B)
+            crossed[n].append(go(whole, whole, twin))
+
+    def cross(n):
+        landed(seconds[n])
+        whole = part(n, across, B)
+        crossed[n].append(go(whole, whole, twin))
+
+    def apply(n):
+        layer, off = RUNS[n]
+        landed(crossed[n])
+        for core in range(NC):
+            out = jnp.dot(basis_ref[layer], gathered[core, n], preferred_element_type=F32)
+            delta_ref[layer, :, core * HALF + off : core * HALF + off + WIDE] = out.astype(BF)
+
+    stages = (multiply, pass_on, over_z, update, over_x, forward, cross, apply)
+    for tick in range(len(RUNS) + len(stages) - 1):
+        for lag, stage in enumerate(stages):
+            if 0 <= tick - lag < len(RUNS):
+                stage(tick - lag)
+    backs = [
+        go(back_first, new_first_ref.at[:, :, mine], twin),
+        go(back_second, new_second_ref.at[:, :, mine], twin),
+    ]
+    landed(backs)
 
 
 def eliminate(whole):
@@ -100,15 +254,23 @@
 STREAMS = ((0, 1024), (1024, 1536))
 BLOCKS = LAYERS * 10 * B
 FAR = NY - 1
+SPLIT, EXTRA = 1024, 256
+KEPT = SPLIT + EXTRA
+PARTS = ((KEPT, OWN - KEPT), (0, KEPT))
 
 
 def rows_at(start, size):
     return pl.ds(pl.multiple_of(start, 8), size)
 
 
-def front_kernel(
+def refresh_kernel(
     omega_hbm,
     grads_hbm,
+    first_ref,
+    second_ref,
+    new_first_ref,
+    new_second_ref,
+    delta_ref,
     summed_ref,
     basis_ref,
     panel_ref,
@@ -118,9 +280,12 @@
     omega_ref,
     grads,
     omegas,
-    relay_in,
-    joint,
-    near_in,
+    relay_a,
+    relay_b,
+    joint_a,
+    joint_b,
+    near_a,
+    near_b,
     partial,
     part,
     rs_buf,
@@ -134,6 +299,7 @@
     y_buf,
     sems,
     local_sems,
+    *tail_scratch,
 ):
     spot = place()
     y, x, z, c = spot
@@ -162,19 +328,23 @@
         for copy in copies:
             copy.wait_recv()
 
+    twin_basis, twin_summed, twin_first, twin_second = tail_scratch[:4]
+    other = span((1 - c) * HALF, HALF)
+    relay_in, joint, near_in = (relay_a, relay_b), (joint_a, joint_b), (near_a, near_b)
     relays, nears = [None] * 2, [None] * 2
 
     SUB = ROWS // 2
 
     def columns(part_of, k):
-        return span(((y + k) % NY) * OWN + (1 - part_of) * HALF, HALF)
+        off, width = PARTS[part_of]
+        return pl.ds(pl.multiple_of(((y + k) % NY) * OWN + off, 2 * B), width)
 
     def launch(part_of):
         relays[part_of] = [
             [
                 go(
                     grads_hbm.at[n, pl.ds(r * SUB, SUB), columns(part_of, 2)],
-                    relay_in.at[part_of, n, pl.ds(r * SUB, SUB), :],
+                    relay_in[part_of].at[n, pl.ds(r * SUB, SUB), :],
                     near_y[2 * n],
                 )
                 for n in range(2)
@@ -188,8 +358,8 @@
                 copy.wait_send()
                 sent.append(id(copy))
         nears[part_of] = [
-            go(grads_hbm.at[1, :, columns(part_of, 1)], near_in.at[part_of, 0, 1], near_y[0]),
-            go(grads_hbm.at[0, :, columns(part_of, 3)], near_in.at[part_of, 1, 0], near_y[2]),
+            go(grads_hbm.at[1, :, columns(part_of, 1)], near_in[part_of].at[0, 1], near_y[0]),
+            go(grads_hbm.at[0, :, columns(part_of, 3)], near_in[part_of].at[1, 0], near_y[2]),
         ]
 
     def in_rows(first_row, count_rows, work):
@@ -200,33 +370,41 @@
         lax.fori_loop(0, count_rows // 32, body, 0)
 
     def combine(part_of):
-        off = (1 - part_of) * HALF
+        off, width = PARTS[part_of]
         for r in range(2):
             for n, k in ((0, 1), (1, 3)):
                 relays[part_of][r][n].wait_recv()
 
                 def work(at):
-                    own_term = grads[k, n, at, off : off + HALF].astype(F32)
-                    joint[part_of, n, at, :] = (own_term + relay_in[part_of, n, at, :].astype(F32)).astype(BF)
+                    own_term = grads[k, n, at, off : off + width].astype(F32)
+                    joint[part_of][n, at, :] = (own_term + relay_in[part_of][n, at, :].astype(F32)).astype(BF)
 
                 in_rows(r * SUB, SUB, work)
                 at = pl.ds(r * SUB, SUB)
-                nears[part_of].append(go(joint.at[part_of, n, at, :], near_in.at[part_of, n, n, at, :], near_y[k - 1]))
+                nears[part_of].append(
+                    go(joint[part_of].at[n, at, :], near_in[part_of].at[n, n, at, :], near_y[k - 1])
+                )
 
     def finish_sum(part_of):
-        off = (1 - part_of) * HALF
+        off, width = PARTS[part_of]
         landed(nears[part_of])
 
         def work(at):
             for n in range(LAYERS):
-                out = grads[0, n, at, off : off + HALF].astype(F32) + near_in[part_of, 0, n, at, :].astype(F32)
-                summed_ref[n, at, off : off + HALF] = (out + near_in[part_of, 1, n, at, :].astype(F32)).astype(BF)
+                out = grads[0, n, at, off : off + width].astype(F32) + near_in[part_of][0, n, at, :].astype(F32)
+                summed_ref[n, at, off : off + width] = (out + near_in[part_of][1, n, at, :].astype(F32)).astype(BF)
 
         in_rows(0, ROWS, work)
 
     strip_at = span(x * 256 + c * B + z * 16, 16)
     slices = [go(omega_hbm.at[strip_at, :], omegas.at[FAR - k, strip_at, :], near_y[k - 1]) for k in range(1, NY)]
+    extra_at = rows_at(SPLIT + c * B + z * 16, 16)
+    extras = [go(omega_hbm.at[extra_at, :], omegas.at[FAR - k, extra_at, :], near_y[k - 1]) for k in range(1, NY)]
     launch(0)
+    moments = [
+        go(first_ref.at[:, :, other], twin_first, twin),
+        go(second_ref.at[:, :, other], twin_second, twin),
+    ]
 
     def block(s, which, start, size):
         return omegas.at[s, pl.ds(pl.multiple_of(which * 256 + c * B + start, size), size), :]
@@ -236,10 +414,13 @@
         slices[FAR - 1 - s].wait_recv()
         piece = omegas.at[s, strip_at, :]
         flights.append([go(piece, piece, peer) for peer in near_z])
+    landed(extras)
+    piece = omegas.at[:, extra_at, :]
+    extras = [go(piece, piece, peer) for peer in near_z]
     for load in loads:
         load.wait()
     for n in range(LAYERS):
-        partial[n] = jnp.dot(grads[0, n, :, :HALF], omega_ref[:HALF, :], preferred_element_type=F32)
+        partial[n] = jnp.dot(grads[0, n, :, :KEPT], omega_ref[:KEPT, :], preferred_element_type=F32)
     launch_near(0)
     up, down = near_x[0], near_x[2]
     above, below, across = (x + 1) % NX, (x + NX - 1) % NX, (x + 2) % NX
@@ -262,6 +443,9 @@
         for which in (below, above):
             whole = block(s, which, 0, B)
             crossed[s].append(go(whole, whole, twin))
+    landed(extras)
+    piece = omegas.at[:, rows_at(SPLIT + c * B, B), :]
+    crossed[0].append(go(piece, piece, twin))
     for s in range(FAR):
         landed(seconds[s])
         whole = block(s, across, 0, B)
@@ -269,10 +453,10 @@
     for s in range(FAR):
         landed(crossed[s])
         for n in range(LAYERS):
-            partial[n] += jnp.dot(grads[s + 1, n, :, :HALF], omegas[s], preferred_element_type=F32)
+            partial[n] += jnp.dot(grads[s + 1, n, :, :KEPT], omegas[s], preferred_element_type=F32)
     finish_sum(0)
     for n in range(LAYERS):
-        out = partial[n] + jnp.dot(summed_ref[n, :, HALF:], omega_ref[HALF:, :], preferred_element_type=F32)
+        out = partial[n] + jnp.dot(summed_ref[n, :, KEPT:], omega_ref[KEPT:, :], preferred_element_type=F32)
         part[n] = out.astype(BF)
 
     q = ROWS // NY
@@ -413,6 +597,8 @@
         return carry
 
     lax.fori_loop(0, 4, step, 0)
+    finish_sum(1)
+    got = [[go(summed_ref.at[RUNS[r][0], :, cut(1 - c, r)], twin_summed.at[r], twin)] for r in range(len(RUNS))]
     landed(spread)
     for n in range(LAYERS):
         rest = w[n]
@@ -422,33 +608,41 @@
             rest = rest - part.astype(F32)
             basis = basis + lax.dot_general(panel_ref[n], part, NT, preferred_element_type=F32)
         basis_ref[n] = basis.astype(BF)
-    finish_sum(1)
+        got[n].append(go(basis_ref.at[n], twin_basis.at[n], twin))
+    refs = (first_ref, second_ref, new_first_ref, new_second_ref, delta_ref)
+    finish(spot, go, landed, moments, got, refs, (summed_ref, basis_ref, w), tail_scratch)
     for copy in done:
         if id(copy) not in sent:
             copy.wait_send()
 
 
-def front(omega, grads):
-    vmem = pl.BlockSpec(memory_space=pltpu.VMEM)
+def refresh(omega, grads, first, second):
+    vmem, hbm = pl.BlockSpec(memory_space=pltpu.VMEM), pl.BlockSpec(memory_space=pltpu.HBM)
     return pl.pallas_call(
-        front_kernel,
+        refresh_kernel,
         out_shape=(
+            jax.ShapeDtypeStruct((8, LAYERS, OWN), F32),
+            jax.ShapeDtypeStruct((8, LAYERS, OWN), F32),
             jax.ShapeDtypeStruct((LAYERS, ROWS, OWN), BF),
-            jax.ShapeDtypeStruct((LAYERS, ROWS, RANK), BF),
         ),
-        in_specs=[pl.BlockSpec(memory_space=pltpu.HBM)] * 2,
-        out_specs=(vmem, vmem),
+        in_specs=[hbm, hbm, vmem, vmem],
+        out_specs=(vmem,) * 3,
         scratch_shapes=[
+            pltpu.VMEM((LAYERS, ROWS, OWN), BF),
+            pltpu.VMEM((LAYERS, ROWS, RANK), BF),
             pltpu.VMEM((LAYERS, ROWS, RANK), BF),
             pltpu.VMEM((BLOCKS, B), F32),
             pltpu.VMEM((LAYERS, RANK, RANK), F32),
             pltpu.VMEM((LAYERS, B, B), F32),
             pltpu.VMEM((OWN, RANK), BF),
             pltpu.VMEM((NY, LAYERS, ROWS, OWN), BF),
-            pltpu.VMEM((FAR, HALF, RANK), BF),
-            pltpu.VMEM((2, LAYERS, ROWS, HALF), BF),
-            pltpu.VMEM((2, LAYERS, ROWS, HALF), BF),
-            pltpu.VMEM((2, 2, LAYERS, ROWS, HALF), BF),
+            pltpu.VMEM((FAR, KEPT, RANK), BF),
+            pltpu.VMEM((LAYERS, ROWS, OWN - KEPT), BF),
+            pltpu.VMEM((LAYERS, ROWS, KEPT), BF),
+            pltpu.VMEM((LAYERS, ROWS, OWN - KEPT), BF),
+            pltpu.VMEM((LAYERS, ROWS, KEPT), BF),
+            pltpu.VMEM((2, LAYERS, ROWS, OWN - KEPT), BF),
+            pltpu.VMEM((2, LAYERS, ROWS, KEPT), BF),
             pltpu.VMEM((LAYERS, ROWS, RANK), F32),
             pltpu.VMEM((LAYERS, ROWS, RANK), BF),
             pltpu.VMEM((NY - 1, LAYERS, ROWS // NY, RANK), BF),
@@ -460,217 +654,8 @@
             pltpu.VMEM((NZ - 1, BLOCKS // 64, B), F32),
             pltpu.VMEM((BLOCKS // 64, B), F32),
             pltpu.VMEM((NY - 1, BLOCKS // 64, B), F32),
-            pltpu.SemaphoreType.DMA((2, 160)),
+            pltpu.SemaphoreType.DMA((2, 320)),
             pltpu.SemaphoreType.DMA((NY + 1,)),
-        ],
-        compiler_params=pltpu.CompilerParams(collective_id=0, has_side_effects=True, vmem_limit_bytes=50 << 20),
-    )(omega, grads)
-
-
-RUNS = ((0, 0), (1, 0), (0, 512), (1, 512))
-WIDE = 512
-
-
-def tail_kernel(
-    basis_ref,
-    summed_ref,
-    first_ref,
-    second_ref,
-    new_first_ref,
-    new_second_ref,
-    delta_ref,
-    summed,
-    twin_basis,
-    twin_summed,
-    twin_first,
-    twin_second,
-    back_first,
-    back_second,
-    relay_out,
-    relay_in,
-    near_out,
-    near_in,
-    x_own,
-    z_out,
-    z_in,
-    z_own,
-    joined,
-    gathered,
-    sems,
-    local_sems,
-):
-    spot = place()
-    y, x, z, c = spot
-    twin = along("c", spot, 1)
-    up, down = along("x", spot, 1), along("x", spot, NX - 1)
-    near_z = [along("z", spot, k) for k in range(1, NZ)]
-    mine, other = span(c * HALF, HALF), span((1 - c) * HALF, HALF)
-    runs = range(len(RUNS))
-
-    def cut(core, r):
-        return pl.ds(pl.multiple_of(core * HALF + RUNS[r][1], WIDE), WIDE)
-
-    loads = []
-    for r in runs:
-        load = pltpu.make_async_copy(summed_ref.at[RUNS[r][0], :, cut(c, r)], summed.at[r], local_sems.at[r])
-        load.start()
-        loads.append(load)
-    greet([twin, up, down] + near_z)
-    done = []
-    count = [0]
-
-    def go(src, dst, peer):
-        copy = ship(src, dst, sems.at[0, count[0]], sems.at[1, count[0]], peer)
-        count[0] += 1
-        done.append(copy)
-        return copy
-
-    def landed(copies):
-        for copy in copies:
-            copy.wait_recv()
-
-    got = []
-    for r in runs:
-        copies = [go(summed_ref.at[RUNS[r][0], :, cut(1 - c, r)], twin_summed.at[r], twin)]
-        if r < LAYERS:
-            copies.append(go(basis_ref.at[r], twin_basis.at[r], twin))
-        got.append(copies)
-    moments = [
-        go(first_ref.at[:, :, other], twin_first, twin),
-        go(second_ref.at[:, :, other], twin_second, twin),
-    ]
-
-    def product(r, start, size):
-        here, n = span(start, size), RUNS[r][0]
-        out = lax.dot_general(basis_ref[n, :, here], summed[r], TN, preferred_element_type=F32)
-        return out + lax.dot_general(twin_basis[n, :, here], twin_summed[r], TN, preferred_element_type=F32)
-
-    h = B // 2
-    above, below, across = ((x + 1) % NX) * B, ((x + NX - 1) % NX) * B, ((x + 2) % NX) * B
-    relays, nears, spreads, firsts, seconds = {}, {}, {}, {}, {}
-    z_copies, crossed = {}, {}
-    slot = span(x * B + z * 16, 16)
-    ours, theirs = span(c * 8, 8), span((1 - c) * 8, 8)
-
-    def part(n, start, size):
-        return gathered.at[c, n, pl.ds(pl.multiple_of(start, size), size), :]
-
-    def multiply(n):
-        landed(got[n])
-        loads[n].wait()
-        far = product(n, across, B)
-        relay_out[n, 0] = far[:h].astype(BF)
-        relay_out[n, 1] = far[h:].astype(BF)
-        relays[n] = [go(relay_out.at[n, 0], relay_in.at[n, 0], up), go(relay_out.at[n, 1], relay_in.at[n, 1], down)]
-        x_own[n, 1] = product(n, above, B)
-        near_out[n, 0, h:, :] = x_own[n, 1, h:, :].astype(BF)
-        nears[n] = [go(near_out.at[n, 0, pl.ds(h, h), :], near_in.at[n, 0, pl.ds(h, h), :], up)]
-        x_own[n, 2] = product(n, below, B)
-        near_out[n, 1, :h, :] = x_own[n, 2, :h, :].astype(BF)
-        nears[n].append(go(near_out.at[n, 1, pl.ds(0, h), :], near_in.at[n, 1, pl.ds(0, h), :], down))
-        x_own[n, 0] = product(n, x * B, B)
-
-    def pass_on(n):
-        relays[n][0].wait_recv()
-        near_out[n, 0, :h, :] = (x_own[n, 1, :h, :] + relay_in[n, 0].astype(F32)).astype(BF)
-        nears[n].append(go(near_out.at[n, 0, pl.ds(0, h), :], near_in.at[n, 0, pl.ds(0, h), :], up))
-        relays[n][1].wait_recv()
-        near_out[n, 1, h:, :] = (x_own[n, 2, h:, :] + relay_in[n, 1].astype(F32)).astype(BF)
-        nears[n].append(go(near_out.at[n, 1, pl.ds(h, h), :], near_in.at[n, 1, pl.ds(h, h), :], down))
-
-    def over_z(n):
-        landed(nears[n])
-        total = x_own[n, 0] + near_in[n, 0].astype(F32) + near_in[n, 1].astype(F32)
-        x_own[n, 0] = total
-        z_out[n] = total.astype(BF)
-        z_copies[n] = [
-            go(z_out.at[n, span(((z + k) % NZ) * 16, 16), :], z_in.at[n, k - 1], near_z[k - 1]) for k in range(1, NZ)
-        ]
-
-    def adam(projected, first, second):
-        new_first = 0.9 * first + 0.1 * projected
-        new_second = 0.999 * second + 0.001 * projected * projected
-        return new_first, new_second, new_first / (jnp.sqrt(new_second) + 1e-08)
-
-    def update(n):
-        layer, off = RUNS[n]
-        here, there = cut(c, n), pl.ds(off, WIDE)
-        if n == 0:
-            landed(moments)
-        landed(z_copies[n])
-        total = x_own[n, 0, span(z * 16, 16), :]
-        for k in range(1, NZ):
-            total = total + z_in[n, k - 1].astype(F32)
-        z_own[n] = total
-        new_first, new_second, fresh = adam(z_own[n, ours, :], first_ref[:, layer, here], second_ref[:, layer, here])
-        new_first_ref[:, layer, here] = new_first
-        new_second_ref[:, layer, here] = new_second
-        joined[n, ours, :] = fresh
-        new_first, new_second, fresh = adam(z_own[n, theirs, :], twin_first[:, layer, there], twin_second[:, layer, there])
-        back_first[:, layer, there] = new_first
-        back_second[:, layer, there] = new_second
-        joined[n, theirs, :] = fresh
-        gathered[c, n, slot, :] = joined[n].astype(BF)
-        piece = gathered.at[c, n, slot, :]
-        spreads[n] = [go(piece, piece, peer) for peer in near_z]
-
-    def over_x(n):
-        landed(spreads[n])
-        low, high, whole = part(n, x * B, h), part(n, x * B + h, h), part(n, x * B, B)
-        firsts[n] = [go(low, low, up), go(high, high, down), go(high, high, up), go(low, low, down)]
-        crossed[n] = [go(whole, whole, twin)]
-
-    def forward(n):
-        firsts[n][0].wait_recv()
-        low = part(n, below, h)
-        seconds[n] = [go(low, low, up)]
-        firsts[n][1].wait_recv()
-        high = part(n, above + h, h)
-        seconds[n].append(go(high, high, down))
-        landed(firsts[n][2:])
-        for start in (below, above):
-            whole = part(n, start, B)
-            crossed[n].append(go(whole, whole, twin))
-
-    def cross(n):
-        landed(seconds[n])
-        whole = part(n, across, B)
-        crossed[n].append(go(whole, whole, twin))
-
-    def apply(n):
-        layer, off = RUNS[n]
-        landed(crossed[n])
-        for core in range(NC):
-            out = jnp.dot(basis_ref[layer], gathered[core, n], preferred_element_type=F32)
-            delta_ref[layer, :, core * HALF + off : core * HALF + off + WIDE] = out.astype(BF)
-
-    stages = (multiply, pass_on, over_z, update, over_x, forward, cross, apply)
-    for tick in range(len(RUNS) + len(stages) - 1):
-        for lag, stage in enumerate(stages):
-            if 0 <= tick - lag < len(RUNS):
-                stage(tick - lag)
-    backs = [
-        go(back_first, new_first_ref.at[:, :, mine], twin),
-        go(back_second, new_second_ref.at[:, :, mine], twin),
-    ]
-    landed(backs)
-    for copy in done:
-        copy.wait_send()
-
-
-def tail(basis, summed, first, second):
-    vmem = pl.BlockSpec(memory_space=pltpu.VMEM)
-    return pl.pallas_call(
-        tail_kernel,
-        out_shape=(
-            jax.ShapeDtypeStruct((8, LAYERS, OWN), F32),
-            jax.ShapeDtypeStruct((8, LAYERS, OWN), F32),
-            jax.ShapeDtypeStruct((LAYERS, ROWS, OWN), BF),
-        ),
-        in_specs=[vmem, pl.BlockSpec(memory_space=pl.ANY), vmem, vmem],
-        out_specs=(vmem,) * 3,
-        scratch_shapes=[
-            pltpu.VMEM((4, ROWS, WIDE), BF),
             pltpu.VMEM((LAYERS, ROWS, RANK), BF),
             pltpu.VMEM((4, ROWS, WIDE), BF),
             pltpu.VMEM((8, LAYERS, HALF), F32),
@@ -681,22 +666,18 @@
             pltpu.VMEM((4, 2, B // 2, WIDE), BF),
             pltpu.VMEM((4, 2, B, WIDE), BF),
             pltpu.VMEM((4, 2, B, WIDE), BF),
-            pltpu.VMEM((4, 3, B, WIDE), F32),
             pltpu.VMEM((4, B, WIDE), BF),
             pltpu.VMEM((4, NZ - 1, 16, WIDE), BF),
             pltpu.VMEM((4, 16, WIDE), F32),
             pltpu.VMEM((4, 16, WIDE), F32),
             pltpu.VMEM((NC, 4, RANK, WIDE), BF),
-            pltpu.SemaphoreType.DMA((2, 144)),
-            pltpu.SemaphoreType.DMA((4,)),
         ],
-        compiler_params=pltpu.CompilerParams(collective_id=1, has_side_effects=True, vmem_limit_bytes=48 << 20),
-    )(basis, summed, first, second)
+        compiler_params=pltpu.CompilerParams(collective_id=0, has_side_effects=True, vmem_limit_bytes=50 << 20),
+    )(omega, grads, first, second)
 
 
 def local(grad_parts, omega, first_moment, second_moment):
-    summed, basis = front(omega, grad_parts[0])
-    return tail(basis, summed, first_moment, second_moment)
+    return refresh(omega, grad_parts[0], first_moment, second_moment)
 
 
 def solution(mesh):

time: 174 us -> 165 us (0.948)
  Pallas kernels: 171 us -> 160 us
  local copies, waits for them, and re-layouts: 2.64 us -> 4.43 us
    pallas_call x2 -> x1, Pallas kernels: 171 us -> 160 us  [refresh(): pl.pallas_call(refresh_kernel, out_shape=(jax.ShapeDtypeStruct((8, LAYERS...]
    unnamed x7, local copies, waits for them, and re-layouts: 2.64 us -> 4.43 us
where the time goes in v6:
time: 165 us
  Pallas kernels  160 us (97%)
  local copies, waits for them, and re-layouts  4.43 us (3%)
    pallas_call x1, Pallas kernels, refresh(): pl.pallas_call(refresh_kernel, out_shape=(jax.ShapeDtypeStruct((8, LAYERS...  160 us
    unnamed x7, local copies, waits for them, and re-layouts  4.43 us

profile of v6, /device:TPU:1, one launch (start us, length us, event | category | flops | bytes accessed | tf_op | source)
XLA Modules:
  0.0 165.3 jit_solution(17818838557995131516)
XLA Ops:
  0.6 0.0 copy-start
  0.6 0.9 copy-done
  1.5 0.0 copy-start.1
  1.5 0.9 copy-done.1
  2.4 160.2 %shard_map.67 = (f32[8,2,2048]{2,1,0:T(2,128)S(1)}, f32[8,2,2048]{2,1,0:T(2,128)S(1)}, bf16[2,256,2048]{2,1,0:T(8,128)(2,1)S(1)}) custom-call(bf16[2048,512]{1,0:T(8,128)(2,1)} %omega_hbm.1, bf16[2,256,8192]{2,1,0:T(8,128)(2,1)} %bitcast.1, f32[8,2,2048]{2,1,0:T(2,128)S(1)} %copy-done, f32[8,2,2048]{2,1,0:T(2,128)S(1)} %copy-done.1), custom_call_target="tpu_custom_call" | custom-call | tf_op jit(solution)/shard_map/pallas_call | solution.py:621
  162.7 0.7 copy.10
  163.3 0.7 copy.11
  164.0 1.3 copy.12
Async XLA Ops:
  0.6 0.9 copy-start
  1.5 0.9 copy-start.1

commit v7 on v6

--- a/solution.py
+++ b/solution.py
@@ -676,8 +676,28 @@
     )(omega, grads, first, second)
 
 
+def store_kernel(*refs):
+    sources, targets, sems = refs[:3], refs[3:6], refs[6]
+    copies = [pltpu.make_async_copy(sources[i], targets[i], sems.at[i]) for i in range(3)]
+    for copy in copies:
+        copy.start()
+    for copy in copies:
+        copy.wait()
+
+
+def store(*results):
+    anywhere = pl.BlockSpec(memory_space=pl.ANY)
+    return pl.pallas_call(
+        store_kernel,
+        out_shape=tuple(jax.ShapeDtypeStruct(r.shape, r.dtype) for r in results),
+        in_specs=[pl.BlockSpec(memory_space=pltpu.VMEM)] * 3,
+        out_specs=(anywhere,) * 3,
+        scratch_shapes=[pltpu.SemaphoreType.DMA((3,))],
+    )(*results)
+
+
 def local(grad_parts, omega, first_moment, second_moment):
-    return refresh(omega, grad_parts[0], first_moment, second_moment)
+    return store(*refresh(omega, grad_parts[0], first_moment, second_moment))
 
 
 def solution(mesh):

time: 165 us -> 169 us (1.024)
  Pallas kernels: 160 us -> 163 us
    pallas_call x0 -> x1, Pallas kernels: none -> 3.18 us  [store(): pl.pallas_call(store_kernel, out_shape=tuple((jax.ShapeDtypeStruct(r.shap...]
    unnamed x7 -> x10, local copies, waits for them, and re-layouts: 4.43 us -> 4.43 us
where the time goes in v7:
time: 169 us
  Pallas kernels  163 us (96%)
  local copies, waits for them, and re-layouts  4.43 us (3%)
    pallas_call x1, Pallas kernels, refresh(): pl.pallas_call(refresh_kernel, out_shape=(jax.ShapeDtypeStruct((8, LAYERS...  160 us
    unnamed x10, local copies, waits for them, and re-layouts  4.43 us

profile of v7, /device:TPU:1, one launch (start us, length us, event | category | flops | bytes accessed | tf_op | source)
XLA Modules:
  0.0 168.6 jit_solution(2620966030168726484)
XLA Ops:
  0.6 0.0 copy-start.1
  0.6 0.9 copy-done.1
  1.5 0.0 copy-start.2
  1.5 0.9 copy-done.2
  2.4 160.2 %shard_map.67 = (f32[8,2,2048]{2,1,0:T(2,128)S(1)}, f32[8,2,2048]{2,1,0:T(2,128)S(1)}, bf16[2,256,2048]{2,1,0:T(8,128)(2,1)S(1)}) custom-call(bf16[2048,512]{1,0:T(8,128)(2,1)} %omega_hbm.1, bf16[2,256,8192]{2,1,0:T(8,128)(2,1)} %bitcast.1, f32[8,2,2048]{2,1,0:T(2,128)S(1)} %copy-done.1, f32[8,2,2048]{2,1,0:T(2,128)S(1)} %copy-done.2), custom_call_target="tpu_custom_call" | custom-call | tf_op jit(solution)/shard_map/pallas_call | solution.py:621
  162.7 0.0 copy-start
  162.7 1.3 copy-done
  164.0 0.0 copy-start.3
  164.0 0.6 copy-done.3
  164.7 0.0 copy-start.4
  164.7 0.6 copy-done.4
  165.3 3.2 %shard_map.68 = (f32[8,2,2048]{2,1,0:T(2,128)}, f32[8,2,2048]{2,1,0:T(2,128)}, bf16[2,256,2048]{2,1,0:T(8,128)(2,1)}) custom-call(f32[8,2,2048]{2,1,0:T(2,128)} %copy-done.3, f32[8,2,2048]{2,1,0:T(2,128)} %copy-done.4, bf16[2,256,2048]{2,1,0:T(8,128)(2,1)} %copy-done), custom_call_target="tpu_custom_call" | custom-call | tf_op jit(solution)/shard_map/pallas_call | solution.py:690
Async XLA Ops:
  0.6 0.9 copy-start.1
  1.5 0.9 copy-start.2
  162.7 1.3 copy-start
  164.0 0.7 copy-start.3
  164.7 0.6 copy-start.4
